TPU v7x, 128 devices: a whole 4x4x4 slice. The times are simulated.
128 devices in a mesh: lon: 32 (over y, z, core), lat: 4 (over x).
Axes of the slice: x: 4, y: 4, z: 4, core: 2. Of those that a mesh axis runs over, the one named last changes fastest.
Arguments:
- kappa_sq: float32 [2048, 2048], P('lon', 'lat'), may hold values from 0.05 to 1
- prior_scale: float32 [2048, 2048], P('lon', 'lat'), may hold values from 0.02 to 0.2
- templates: bfloat16 [64, 128, 256], replicated, may hold values from -0.375 to 0.375
- block_counts: int32 [128], P(('lon', 'lat')), may hold values from 1 to 128, 8192 in all
- anchor_lon: int32 [32, 512], P('lon', 'lat'), may hold values from 0 to 48
- anchor_lat: int32 [32, 512], P('lon', 'lat'), may hold values from 0 to 496
- template_ids: int32 [32, 512], P('lon', 'lat'), may hold values from 0 to 63
- readings: float32 [32, 512, 128], P('lon', 'lat'), may hold values from -12 to 12
- noise_prec: float32 [32, 512, 128], P('lon', 'lat'), may hold values from 0.3 to 3
Outputs:
- solution_field: float32 [2048, 2048], P('lon', 'lat')
- residual: float32 [2048, 2048], P('lon', 'lat')
Inputs may be any that keep to these rules, and one draw needn't show every extreme that they name: `block_counts`: slots of a tile at or past its count are ignored; some tile lists exactly 128 blocks. `anchor_lon`: every patch lies inside its own tile. `anchor_lat`: every patch lies inside its own tile.
All inputs are finite; a program needn't handle non-finite values.
Results may differ from a plain program's by a relative error of at most 0.0003.
Values sent between devices are 32-bit elements; how exact they have to be, the bound alone decides.
A program may use at most 64 MiB of HBM per device.

v0:
```python
import jax
import jax.numpy as jnp
from jax import lax
from jax.sharding import PartitionSpec as P

PSIDE = 16
ITERS = 3


def extended(cells, sides, width, closed):
    for axis, dim in sides:
        count = lax.axis_size(axis)
        ends = count if closed else count - 1
        head = lax.slice_in_dim(cells, 0, width, axis=dim)
        tail = lax.slice_in_dim(cells, cells.shape[dim] - width, cells.shape[dim], axis=dim)
        cells = jnp.concatenate(
            [
                lax.ppermute(tail, axis, [(i, (i + 1) % count) for i in range(ends)]),
                cells,
                lax.ppermute(head, axis, [((i + 1) % count, i) for i in range(ends)]),
            ],
            axis=dim,
        )
    return cells


def narrow_stencil(field, coeff):
    along = extended(field, (("lon", 0),), 1, True)
    across = extended(field, (("lat", 1),), 1, False)
    return (coeff + 4.0) * field - (along[2:] + along[:-2] + across[:, 2:] + across[:, :-2])


def squares(vector):
    return lax.psum(jnp.sum(vector * vector), ("lon", "lat"))


def selectors(start_lon, start_lat, cells_lon, cells_lat, side):
    offset = jnp.arange(side, dtype=jnp.int32)
    lon_pos = jnp.arange(cells_lon, dtype=jnp.int32)
    lat_pos = jnp.arange(cells_lat, dtype=jnp.int32)
    lon_sel = (lon_pos[None, :, None] == start_lon[:, None, None] + offset[None, None, :]).astype(
        jnp.float32
    )
    lat_sel = (lat_pos[None, :, None] == start_lat[:, None, None] + offset[None, None, :]).astype(
        jnp.float32
    )
    return (lon_sel, lat_sel)


def read_patches(field, lon_sel, lat_sel):
    rows = jnp.einsum("bxa,xy->bay", lon_sel, field, precision=lax.Precision.HIGHEST)
    patch = jnp.einsum("bay,byc->bac", rows, lat_sel, precision=lax.Precision.HIGHEST)
    return patch.reshape(patch.shape[0], -1)


def write_patches(terms, lon_sel, lat_sel):
    side = lon_sel.shape[2]
    shaped = terms.reshape(terms.shape[0], side, side)
    rows = jnp.einsum("bac,byc->bay", shaped, lat_sel, precision=lax.Precision.HIGHEST)
    return jnp.einsum("bxa,bay->xy", lon_sel, rows, precision=lax.Precision.HIGHEST)


def block_terms(patches, idents, weights, extra, templates, count):
    total = patches.shape[0]
    group = min(64, total)
    kinds = templates.shape[0]
    table = templates.reshape(kinds, -1)
    kind_ids = jnp.arange(kinds, dtype=jnp.int32)

    def one_group(turn, acc):
        start = turn * group
        patch = lax.dynamic_slice_in_dim(patches, start, group, 0)
        ident = lax.dynamic_slice_in_dim(idents, start, group, 0)
        weight = lax.dynamic_slice_in_dim(weights, start, group, 0)
        added = lax.dynamic_slice_in_dim(extra, start, group, 0)
        onehot = (ident[:, None] == kind_ids[None, :]).astype(jnp.bfloat16)
        chosen = jnp.dot(onehot, table, preferred_element_type=jnp.float32).reshape(
            (group,) + templates.shape[1:]
        )
        image = jnp.einsum("gri,gi->gr", chosen, patch, precision=lax.Precision.HIGHEST)
        mixed = weight * image + added
        result = jnp.einsum("gri,gr->gi", chosen, mixed, precision=lax.Precision.HIGHEST)
        return lax.dynamic_update_slice_in_dim(acc, result, start, 0)

    turns = (count + group - 1) // group
    return lax.fori_loop(0, turns, one_group, jnp.zeros(patches.shape, jnp.float32))


def on_device(
    kappa_sq,
    prior_scale,
    templates,
    block_counts,
    anchor_lon,
    anchor_lat,
    template_ids,
    readings,
    noise_prec,
):
    cells_lon, cells_lat = kappa_sq.shape
    slots_all = template_ids.shape[1]
    patch_cells = templates.shape[2]
    count = block_counts[0]
    slots = jnp.arange(slots_all, dtype=jnp.int32)
    live = slots < count
    idents = jnp.where(live, template_ids[0], -1)
    weights = jnp.where(live[:, None], noise_prec[0], 0.0)
    weighted = weights * readings[0]
    zero_patch = jnp.zeros((slots_all, patch_cells), jnp.float32)
    zero_extra = jnp.zeros_like(weights)
    devices = lax.axis_size(("lon", "lat"))
    share = slots_all // devices

    def dealt(array):
        return jnp.swapaxes(array.reshape((share, devices) + array.shape[1:]), 0, 1)

    lon_sel, lat_sel = selectors(
        dealt(anchor_lon[0]).reshape(-1),
        dealt(anchor_lat[0]).reshape(-1),
        cells_lon,
        cells_lat,
        PSIDE,
    )
    idents_in = lax.all_to_all(
        dealt(idents), ("lon", "lat"), split_axis=0, concat_axis=0, tiled=True
    ).reshape(-1)
    weights_in, weighted_in = (
        lax.all_to_all(dealt(weights), ("lon", "lat"), split_axis=0, concat_axis=0, tiled=True),
        lax.all_to_all(dealt(weighted), ("lon", "lat"), split_axis=0, concat_axis=0, tiled=True),
    )
    weights_in = weights_in.reshape(slots_all, -1)
    weighted_in = weighted_in.reshape(slots_all, -1)
    live_flag = (idents_in >= 0).astype(jnp.int32)
    live_in = jnp.sum(live_flag)
    position = jnp.where(
        live_flag > 0, jnp.cumsum(live_flag) - 1, live_in + jnp.cumsum(1 - live_flag) - 1
    )
    placing = slots[:, None] == position[None, :]
    place_float = placing.astype(jnp.float32)
    idents_packed = jnp.dot(placing.astype(jnp.int32), idents_in)

    def pack(array):
        return jnp.dot(place_float, array, precision=lax.Precision.HIGHEST)

    def unpack(array):
        return jnp.dot(place_float.T, array, precision=lax.Precision.HIGHEST)

    weights_packed = pack(weights_in)

    def returned(packed):
        sent = unpack(packed).reshape(devices, share, patch_cells)
        return lax.all_to_all(
            sent, ("lon", "lat"), split_axis=0, concat_axis=0, tiled=True
        ).reshape(slots_all, patch_cells)

    right_terms = returned(
        block_terms(
            zero_patch, idents_packed, weights_packed, pack(weighted_in), templates, live_in
        )
    )

    def spread_terms(terms):
        return write_patches(terms, lon_sel, lat_sel)

    right = spread_terms(right_terms)
    solution_field = jnp.zeros_like(right)
    residual = right
    direction = right
    norm_now = squares(residual)
    for turn in range(ITERS):
        observe_sent = read_patches(direction, lon_sel, lat_sel).reshape(
            devices, share, patch_cells
        )
        got = lax.all_to_all(
            observe_sent, ("lon", "lat"), split_axis=0, concat_axis=0, tiled=True
        ).reshape(slots_all, patch_cells)
        image = narrow_stencil(
            prior_scale * narrow_stencil(direction, kappa_sq), kappa_sq
        ) + spread_terms(
            returned(
                block_terms(
                    pack(got), idents_packed, weights_packed, zero_extra, templates, live_in
                )
            )
        )
        alpha = norm_now / lax.psum(jnp.sum(direction * image), ("lon", "lat"))
        solution_field = solution_field + alpha * direction
        residual = residual - alpha * image
        norm_next = squares(residual)
        direction = residual + norm_next / norm_now * direction
        norm_now = norm_next
    return (solution_field, residual)


def solution(mesh):
    return jax.shard_map(
        on_device,
        mesh=mesh,
        in_specs=(
            P("lon", "lat"),
            P("lon", "lat"),
            P(),
            P(("lon", "lat")),
            P("lon", "lat"),
            P("lon", "lat"),
            P("lon", "lat"),
            P("lon", "lat", None),
            P("lon", "lat", None),
        ),
        out_specs=(P("lon", "lat"), P("lon", "lat")),
        check_vma=False,
    )
```

profile of v0, /device:TPU:1, one launch (start us, length us, event | category | flops | bytes accessed | tf_op | source)
XLA Modules:
  0.0 721.6 jit_solution(2078949896948826403)
XLA Ops:
  2.7 11.5 %all-to-all-start = ((s32[128,1,1]{2,1,0:T(1,128)}), s32[128,1,1]{2,1,0:T(1,128)S(1)}, u32[]{:S(2)}, u32[]{:S(2)}) async-start(s32[128,1,1]{2,1,0:T(1,128)} %copy.50), calls=%async_computation | async-start | bytes 131072 | tf_op jit(solution)/shard_map/all_to_all | solution.py:124
  24.0 9.7 %all-to-all-start.1 = ((f32[128,1,128]{2,1,0:T(1,128)}), f32[128,1,128]{2,1,0:T(1,128)S(1)}, u32[]{:S(2)}, u32[]{:S(2)}) async-start(f32[128,1,128]{2,1,0:T(1,128)} %get-tuple-element.316), calls=%async_computation.1 | async-start | bytes 131072 | tf_op jit(solution)/shard_map/all_to_all | solution.py:128
  43.6 7.4 %all-to-all-start.2 = ((f32[128,1,128]{2,1,0:T(1,128)}), f32[128,1,128]{2,1,0:T(1,128)S(1)}, u32[]{:S(2)}, u32[]{:S(2)}) async-start(f32[128,1,128]{2,1,0:T(1,128)} %get-tuple-element.315), calls=%async_computation.2 | async-start | bytes 131072 | tf_op jit(solution)/shard_map/all_to_all | solution.py:129
  51.2 9.6 %all-to-all-done.2 = f32[128,1,128]{2,1,0:T(1,128)S(1)} async-done(((f32[128,1,128]{2,1,0:T(1,128)}), f32[128,1,128]{2,1,0:T(1,128)S(1)}, u32[]{:S(2)}, u32[]{:S(2)}) %all-to-all-start.2) | async-done | bytes 65568 | tf_op jit(solution)/shard_map/all_to_all | solution.py:129
  61.0 44.5 %while.44 = (s32[]{:T(128)}, f32[128,256]{1,0:T(8,128)S(1)}, s32[]{:T(128)}, s32[128]{0:T(128)S(1)}, bf16[64,32768]{1,0:T(8,128)(2,1)}, /*index=5*/f32[128,128]{...) while((s32[]{:T(128)}, f32[128,256]{1,0:T(8,128)S(1)}, ...), condition=%wide.region_4.5_spmd.clone, body=%wide.region_3.4_spmd.clone.sunk | while | flops 318787584 | bytes 46531496 | solution.py:86
  110.5 10.1 %all-to-all-done.3 = f32[128,1,256]{2,1,0:T(1,128)S(1)} async-done(((f32[128,1,256]{2,1,0:T(1,128)}), f32[128,1,256]{2,1,0:T(1,128)S(1)}, u32[]{:S(2)}, u32[]{:S(2)}) %all-to-all-start.3) | async-done | bytes 131104 | tf_op jit(solution)/shard_map/all_to_all | solution.py:152
  157.7 36.1 %while.45 = (s32[]{:T(128)}, f32[128,256]{1,0:T(8,128)S(1)}, s32[]{:T(128)}, s32[128]{0:T(128)S(1)}, bf16[64,32768]{1,0:T(8,128)(2,1)}, /*index=5*/f32[128,128]{...) while((s32[]{:T(128)}, f32[128,256]{1,0:T(8,128)S(1)}, ...), condition=%wide.region_8.9_spmd.clone, body=%wide.region_7.8_spmd.clone.sunk | while | flops 318779392 | bytes 46695336 | solution.py:86
  164.0 7.1 fusion.218
  181.7 7.1 fusion.218
  201.1 8.1 %all-to-all-done.5 = f32[128,1,256]{2,1,0:T(1,128)S(1)} async-done(((f32[128,1,256]{2,1,0:T(1,128)}), f32[128,1,256]{2,1,0:T(1,128)S(1)}, u32[]{:S(2)}, u32[]{:S(2)}) %all-to-all-start.5) | async-done | bytes 131104 | tf_op jit(solution)/shard_map/all_to_all | solution.py:152
  217.0 62.9 %all-reduce = (f32[]{:T(128)}, f32[]{:T(128)}) all-reduce(f32[]{:T(128)} %get-tuple-element.247, f32[]{:T(128)} %get-tuple-element.246), channel_id=1, replica_groups=mesh['lon'=32,'lat'=4] {'lon','lat'}, use_global_device_ids=true, to_apply=%region_6.7 | all-reduce | flops 2 | bytes 16 | tf_op jit(solution)/shard_map/psum | solution.py:34
  281.8 62.8 %psum.44 = f32[]{:T(128)} all-reduce(f32[]{:T(128)} %multiply_reduce_fusion.3), channel_id=1, replica_groups=mesh['lon'=32,'lat'=4] {'lon','lat'}, use_global_device_ids=true, to_apply=%region_12.13 | all-reduce | flops 1 | bytes 8 | tf_op jit(solution)/shard_map/psum | solution.py:34
  359.4 7.7 %all-to-all-start.6 = ((f32[128,1,256]{2,1,0:T(1,128)}), f32[128,1,256]{2,1,0:T(1,128)S(1)}, u32[]{:S(2)}, u32[]{:S(2)}) async-start(f32[128,1,256]{2,1,0:T(1,128)} %copy.66), calls=%async_computation.6 | async-start | bytes 262144 | tf_op jit(solution)/shard_map/all_to_all | solution.py:174
  377.5 35.8 %while.46 = (s32[]{:T(128)}, f32[128,256]{1,0:T(8,128)S(1)}, s32[]{:T(128)}, s32[128]{0:T(128)S(1)}, bf16[64,32768]{1,0:T(8,128)(2,1)}, /*index=5*/f32[128,128]{...) while((s32[]{:T(128)}, f32[128,256]{1,0:T(8,128)S(1)}, ...), condition=%wide.region_14.15_spmd.clone, body=%wide.region_13.14_spmd.clone.sunk | while | flops 318779392 | bytes 46695336 | solution.py:86
  383.6 7.1 fusion.226
  401.3 7.1 fusion.226
  420.6 8.1 %all-to-all-done.7 = f32[128,1,256]{2,1,0:T(1,128)S(1)} async-done(((f32[128,1,256]{2,1,0:T(1,128)}), f32[128,1,256]{2,1,0:T(1,128)S(1)}, u32[]{:S(2)}, u32[]{:S(2)}) %all-to-all-start.7) | async-done | bytes 131104 | tf_op jit(solution)/shard_map/all_to_all | solution.py:152
  436.5 62.8 %psum.45 = f32[]{:T(128)} all-reduce(f32[]{:T(128)} %get-tuple-element.312), channel_id=1, replica_groups=mesh['lon'=32,'lat'=4] {'lon','lat'}, use_global_device_ids=true, to_apply=%region_16.17 | all-reduce | flops 1 | bytes 8 | tf_op jit(solution)/shard_map/psum | solution.py:186
  501.2 62.8 %psum.46 = f32[]{:T(128)} all-reduce(f32[]{:T(128)} %get-tuple-element.310), channel_id=1, replica_groups=mesh['lon'=32,'lat'=4] {'lon','lat'}, use_global_device_ids=true, to_apply=%region_18.19 | all-reduce | flops 1 | bytes 8 | tf_op jit(solution)/shard_map/psum | solution.py:34
  578.8 7.7 %all-to-all-start.8 = ((f32[128,1,256]{2,1,0:T(1,128)}), f32[128,1,256]{2,1,0:T(1,128)S(1)}, u32[]{:S(2)}, u32[]{:S(2)}) async-start(f32[128,1,256]{2,1,0:T(1,128)} %copy.73), calls=%async_computation.8 | async-start | bytes 262144 | tf_op jit(solution)/shard_map/all_to_all | solution.py:174
  596.9 35.7 %while.47 = (s32[]{:T(128)}, f32[128,256]{1,0:T(8,128)S(1)}, s32[]{:T(128)}, s32[128]{0:T(128)S(1)}, bf16[64,32768]{1,0:T(8,128)(2,1)}, /*index=5*/f32[128,128]{...) while((s32[]{:T(128)}, f32[128,256]{1,0:T(8,128)S(1)}, ...), condition=%wide.region_20.21_spmd.clone, body=%wide.region_19.20_spmd.clone.sunk | while | flops 318779392 | bytes 46695336 | solution.py:86
  620.7 7.1 fusion.234
  639.8 8.1 %all-to-all-done.9 = f32[128,1,256]{2,1,0:T(1,128)S(1)} async-done(((f32[128,1,256]{2,1,0:T(1,128)}), f32[128,1,256]{2,1,0:T(1,128)S(1)}, u32[]{:S(2)}, u32[]{:S(2)}) %all-to-all-start.9) | async-done | bytes 131104 | tf_op jit(solution)/shard_map/all_to_all | solution.py:152
  655.7 62.8 %psum.47 = f32[]{:T(128)} all-reduce(f32[]{:T(128)} %get-tuple-element.308), channel_id=1, replica_groups=mesh['lon'=32,'lat'=4] {'lon','lat'}, use_global_device_ids=true, to_apply=%region_22.23 | all-reduce | flops 1 | bytes 8 | tf_op jit(solution)/shard_map/psum | solution.py:186
  (206 shorter events, 262.9 us)
Async XLA Ops:
  2.7 21.3 %all-to-all-start = ((s32[128,1,1]{2,1,0:T(1,128)}), s32[128,1,1]{2,1,0:T(1,128)S(1)}, u32[]{:S(2)}, u32[]{:S(2)}) async-start(s32[128,1,1]{2,1,0:T(1,128)} %copy.50), calls=%async_computation | async-start | bytes 131072 | tf_op jit(solution)/shard_map/all_to_all | solution.py:124
  24.0 19.6 %all-to-all-start.1 = ((f32[128,1,128]{2,1,0:T(1,128)}), f32[128,1,128]{2,1,0:T(1,128)S(1)}, u32[]{:S(2)}, u32[]{:S(2)}) async-start(f32[128,1,128]{2,1,0:T(1,128)} %get-tuple-element.316), calls=%async_computation.1 | async-start | bytes 131072 | tf_op jit(solution)/shard_map/all_to_all | solution.py:128
  43.6 17.2 %all-to-all-start.2 = ((f32[128,1,128]{2,1,0:T(1,128)}), f32[128,1,128]{2,1,0:T(1,128)S(1)}, u32[]{:S(2)}, u32[]{:S(2)}) async-start(f32[128,1,128]{2,1,0:T(1,128)} %get-tuple-element.315), calls=%async_computation.2 | async-start | bytes 131072 | tf_op jit(solution)/shard_map/all_to_all | solution.py:129
  106.6 14.0 %all-to-all-start.3 = ((f32[128,1,256]{2,1,0:T(1,128)}), f32[128,1,256]{2,1,0:T(1,128)S(1)}, u32[]{:S(2)}, u32[]{:S(2)}) async-start(f32[128,1,256]{2,1,0:T(1,128)} %copy.53), calls=%async_computation.3 | async-start | bytes 262144 | tf_op jit(solution)/shard_map/all_to_all | solution.py:152
  132.8 14.6 %collective-permute-start = (f32[1,512]{1,0:T(1,128)S(1)}, f32[1,512]{1,0:T(1,128)S(1)}, u32[]{:S(2)}, u32[]{:S(2)}) collective-permute-start(f32[1,512]{1,0:T(1,128)S(1)} %get-tuple-element.337), channel_id=1, source_target_pairs={{4,0},{8,4},{12,8},{16,12},{20,16},{24,20},{28,24},{32,28},{36,32}... | collective-permute-start | bytes 6152 | tf_op jit(solution)/shard_map/ppermute | solution.py:20
  133.2 14.1 %collective-permute-start.1 = (f32[1,512]{1,0:T(1,128)S(1)}, f32[1,512]{1,0:T(1,128)S(1)}, u32[]{:S(2)}, u32[]{:S(2)}) collective-permute-start(f32[1,512]{1,0:T(1,128)S(1)} %get-tuple-element.338), channel_id=1, source_target_pairs={{0,4},{4,8},{8,12},{12,16},{16,20},{20,24},{24,28},{28,32},{32,36}... | collective-permute-start | bytes 6152 | tf_op jit(solution)/shard_map/ppermute | solution.py:18
  141.1 16.3 %all-to-all-start.4 = ((f32[128,1,256]{2,1,0:T(1,128)}), f32[128,1,256]{2,1,0:T(1,128)S(1)}, u32[]{:S(2)}, u32[]{:S(2)}) async-start(f32[128,1,256]{2,1,0:T(1,128)} %copy.59), calls=%async_computation.4 | async-start | bytes 262144 | tf_op jit(solution)/shard_map/all_to_all | solution.py:174
  147.7 64.6 %collective-permute-start.6 = (f32[64,1]{1,0:T(8,128)S(1)}, f32[64,1]{1,0:T(8,128)S(1)}, u32[]{:S(2)}, u32[]{:S(2)}) collective-permute-start(f32[64,1]{1,0:T(8,128)S(1)} %get-tuple-element.335), channel_id=1, source_target_pairs={{1,0},{2,1},{3,2},{5,4},{6,5},{7,6},{9,8},{10,9},{11,10},{13,12},{... | collective-permute-start | bytes 776 | tf_op jit(solution)/shard_map/ppermute | solution.py:20
  148.9 63.3 %collective-permute-start.7 = (f32[64,1]{1,0:T(8,128)S(1)}, f32[64,1]{1,0:T(8,128)S(1)}, u32[]{:S(2)}, u32[]{:S(2)}) collective-permute-start(f32[64,1]{1,0:T(8,128)S(1)} %get-tuple-element.336), channel_id=1, source_target_pairs={{0,1},{1,2},{2,3},{4,5},{5,6},{6,7},{8,9},{9,10},{10,11},{12,13},{... | collective-permute-start | bytes 776 | tf_op jit(solution)/shard_map/ppermute | solution.py:18
  194.9 14.3 %all-to-all-start.5 = ((f32[128,1,256]{2,1,0:T(1,128)}), f32[128,1,256]{2,1,0:T(1,128)S(1)}, u32[]{:S(2)}, u32[]{:S(2)}) async-start(f32[128,1,256]{2,1,0:T(1,128)} %copy.60), calls=%async_computation.5 | async-start | bytes 262144 | tf_op jit(solution)/shard_map/all_to_all | solution.py:152
  351.1 16.1 %collective-permute-start.8 = (f32[1,512]{1,0:T(1,128)S(1)}, f32[1,512]{1,0:T(1,128)S(1)}, u32[]{:S(2)}, u32[]{:S(2)}) collective-permute-start(f32[1,512]{1,0:T(1,128)S(1)} %get-tuple-element.329), channel_id=1, source_target_pairs={{4,0},{8,4},{12,8},{16,12},{20,16},{24,20},{28,24},{32,28},{36,32}... | collective-permute-start | bytes 6152 | tf_op jit(solution)/shard_map/ppermute | solution.py:20
  351.8 15.4 %collective-permute-start.9 = (f32[1,512]{1,0:T(1,128)S(1)}, f32[1,512]{1,0:T(1,128)S(1)}, u32[]{:S(2)}, u32[]{:S(2)}) collective-permute-start(f32[1,512]{1,0:T(1,128)S(1)} %get-tuple-element.330), channel_id=1, source_target_pairs={{0,4},{4,8},{8,12},{12,16},{16,20},{20,24},{24,28},{28,32},{32,36}... | collective-permute-start | bytes 6152 | tf_op jit(solution)/shard_map/ppermute | solution.py:18
  353.0 14.2 %collective-permute-start.10 = (f32[64,1]{1,0:T(8,128)S(1)}, f32[64,1]{1,0:T(8,128)S(1)}, u32[]{:S(2)}, u32[]{:S(2)}) collective-permute-start(f32[64,1]{1,0:T(8,128)S(1)} %get-tuple-element.331), channel_id=1, source_target_pairs={{1,0},{2,1},{3,2},{5,4},{6,5},{7,6},{9,8},{10,9},{11,10},{13,12},{... | collective-permute-start | bytes 776 | tf_op jit(solution)/shard_map/ppermute | solution.py:20
  359.4 17.8 %all-to-all-start.6 = ((f32[128,1,256]{2,1,0:T(1,128)}), f32[128,1,256]{2,1,0:T(1,128)S(1)}, u32[]{:S(2)}, u32[]{:S(2)}) async-start(f32[128,1,256]{2,1,0:T(1,128)} %copy.66), calls=%async_computation.6 | async-start | bytes 262144 | tf_op jit(solution)/shard_map/all_to_all | solution.py:174
  367.4 64.3 %collective-permute-start.14 = (f32[64,1]{1,0:T(8,128)S(1)}, f32[64,1]{1,0:T(8,128)S(1)}, u32[]{:S(2)}, u32[]{:S(2)}) collective-permute-start(f32[64,1]{1,0:T(8,128)S(1)} %get-tuple-element.327), channel_id=1, source_target_pairs={{1,0},{2,1},{3,2},{5,4},{6,5},{7,6},{9,8},{10,9},{11,10},{13,12},{... | collective-permute-start | bytes 776 | tf_op jit(solution)/shard_map/ppermute | solution.py:20
  368.7 63.0 %collective-permute-start.15 = (f32[64,1]{1,0:T(8,128)S(1)}, f32[64,1]{1,0:T(8,128)S(1)}, u32[]{:S(2)}, u32[]{:S(2)}) collective-permute-start(f32[64,1]{1,0:T(8,128)S(1)} %get-tuple-element.328), channel_id=1, source_target_pairs={{0,1},{1,2},{2,3},{4,5},{5,6},{6,7},{8,9},{9,10},{10,11},{12,13},{... | collective-permute-start | bytes 776 | tf_op jit(solution)/shard_map/ppermute | solution.py:18
  414.4 14.3 %all-to-all-start.7 = ((f32[128,1,256]{2,1,0:T(1,128)}), f32[128,1,256]{2,1,0:T(1,128)S(1)}, u32[]{:S(2)}, u32[]{:S(2)}) async-start(f32[128,1,256]{2,1,0:T(1,128)} %copy.67), calls=%async_computation.7 | async-start | bytes 262144 | tf_op jit(solution)/shard_map/all_to_all | solution.py:152
  570.5 16.1 %collective-permute-start.16 = (f32[1,512]{1,0:T(1,128)S(1)}, f32[1,512]{1,0:T(1,128)S(1)}, u32[]{:S(2)}, u32[]{:S(2)}) collective-permute-start(f32[1,512]{1,0:T(1,128)S(1)} %get-tuple-element.321), channel_id=1, source_target_pairs={{4,0},{8,4},{12,8},{16,12},{20,16},{24,20},{28,24},{32,28},{36,32}... | collective-permute-start | bytes 6152 | tf_op jit(solution)/shard_map/ppermute | solution.py:20
  571.2 15.4 %collective-permute-start.17 = (f32[1,512]{1,0:T(1,128)S(1)}, f32[1,512]{1,0:T(1,128)S(1)}, u32[]{:S(2)}, u32[]{:S(2)}) collective-permute-start(f32[1,512]{1,0:T(1,128)S(1)} %get-tuple-element.322), channel_id=1, source_target_pairs={{0,4},{4,8},{8,12},{12,16},{16,20},{20,24},{24,28},{28,32},{32,36}... | collective-permute-start | bytes 6152 | tf_op jit(solution)/shard_map/ppermute | solution.py:18
  572.4 14.2 %collective-permute-start.18 = (f32[64,1]{1,0:T(8,128)S(1)}, f32[64,1]{1,0:T(8,128)S(1)}, u32[]{:S(2)}, u32[]{:S(2)}) collective-permute-start(f32[64,1]{1,0:T(8,128)S(1)} %get-tuple-element.323), channel_id=1, source_target_pairs={{1,0},{2,1},{3,2},{5,4},{6,5},{7,6},{9,8},{10,9},{11,10},{13,12},{... | collective-permute-start | bytes 776 | tf_op jit(solution)/shard_map/ppermute | solution.py:20
  578.8 17.8 %all-to-all-start.8 = ((f32[128,1,256]{2,1,0:T(1,128)}), f32[128,1,256]{2,1,0:T(1,128)S(1)}, u32[]{:S(2)}, u32[]{:S(2)}) async-start(f32[128,1,256]{2,1,0:T(1,128)} %copy.73), calls=%async_computation.8 | async-start | bytes 262144 | tf_op jit(solution)/shard_map/all_to_all | solution.py:174
  586.9 64.1 %collective-permute-start.22 = (f32[64,1]{1,0:T(8,128)S(1)}, f32[64,1]{1,0:T(8,128)S(1)}, u32[]{:S(2)}, u32[]{:S(2)}) collective-permute-start(f32[64,1]{1,0:T(8,128)S(1)} %get-tuple-element.319), channel_id=1, source_target_pairs={{1,0},{2,1},{3,2},{5,4},{6,5},{7,6},{9,8},{10,9},{11,10},{13,12},{... | collective-permute-start | bytes 776 | tf_op jit(solution)/shard_map/ppermute | solution.py:20
  588.2 62.8 %collective-permute-start.23 = (f32[64,1]{1,0:T(8,128)S(1)}, f32[64,1]{1,0:T(8,128)S(1)}, u32[]{:S(2)}, u32[]{:S(2)}) collective-permute-start(f32[64,1]{1,0:T(8,128)S(1)} %get-tuple-element.320), channel_id=1, source_target_pairs={{0,1},{1,2},{2,3},{4,5},{5,6},{6,7},{8,9},{9,10},{10,11},{12,13},{... | collective-permute-start | bytes 776 | tf_op jit(solution)/shard_map/ppermute | solution.py:18
  633.6 14.3 %all-to-all-start.9 = ((f32[128,1,256]{2,1,0:T(1,128)}), f32[128,1,256]{2,1,0:T(1,128)S(1)}, u32[]{:S(2)}, u32[]{:S(2)}) async-start(f32[128,1,256]{2,1,0:T(1,128)} %copy.74), calls=%async_computation.9 | async-start | bytes 262144 | tf_op jit(solution)/shard_map/all_to_all | solution.py:152
  (13 other events, 210.6 us)
where the time goes:
time: 730 us; the launch traced here: 722 us
  blocking collectives  314 us (43%)
  matrix products  166 us (23%)
  starting transfers between devices  110 us (15%)
  waiting for transfers between devices  60.2 us (8%)
  local copies, waits for them, and re-layouts  38.5 us (5%)
  other arithmetic  12.9 us (2%)
  loops' own time  10.8 us (1%)
  between operations  9.79 us (1%)
    psum x3, blocking collectives, squares(): return lax.psum(jnp.sum(vector * vector), ('lon', 'lat'))  188 us
    psum x2, blocking collectives, on_device(): alpha = norm_now / lax.psum(jnp.sum(direction * image), ('lon', 'lat'))  126 us
    dot_general x8, matrix products, one_group(): jnp.einsum('gri,gi->gr', chosen, patch, precision=lax.Precision.HIGHEST)  57 us
    dot_general x8, matrix products, one_group(): jnp.einsum('gri,gr->gi', chosen, mixed, precision=lax.Precision.HIGHEST)  35.6 us
    all_to_all x4, waiting for transfers between devices, returned(): lax.all_to_all(sent, ('lon', 'lat'), split_axis=0, concat_axis=0, tiled=T...  34.5 us
    ppermute x12, starting transfers between devices, extended(): lax.ppermute(tail, axis, [(i, (i + 1) % count) for i in range(ends)])  29.8 us
    dot_general x8, matrix products, one_group(): jnp.dot(onehot, table, preferred_element_type=jnp.float32)  27.8 us
    all_to_all x3, starting transfers between devices, on_device(): lax.all_to_all(observe_sent, ('lon', 'lat'), split_axis=0, concat_axis=0,...  21.7 us
  transfers between devices with their start and end apart: 34, of which 9 were waited for; matrix products, arithmetic and copies ran while one was open for 19% of the time, Pallas kernels for 0%

commit v1 on v0

v1 whole, which is shorter than its diff:
```python
import functools

import jax
import jax.numpy as jnp
from jax import lax
from jax.experimental import pallas as pl
from jax.experimental.pallas import tpu as pltpu
from jax.sharding import PartitionSpec as P

PSIDE = 16
ITERS = 3
LANES = 128
ROWS = 8
PER_TILE = LANES // PSIDE
F32 = jnp.float32
BF16 = jnp.bfloat16
MESH = pl.DeviceIdType.MESH
NT = (((1,), (1,)), ((), ()))


def split(value):
    high = value.astype(BF16)
    low = (value - high.astype(F32)).astype(BF16)
    return high, low


def block_transpose(value):
    row = lax.broadcasted_iota(jnp.int32, value.shape, 1)
    chunk = lax.broadcasted_iota(jnp.int32, value.shape, 2) // PSIDE
    for k in (4, 2, 1):
        row_bit = (row // k) % 2
        chunk_bit = (chunk // k) % 2
        ahead = pltpu.roll(pltpu.roll(value, ROWS - k, 1), PSIDE * k, 2)
        if k == 4:
            other = ahead
        else:
            behind = pltpu.roll(pltpu.roll(value, k, 1), LANES - PSIDE * k, 2)
            other = jnp.where(row_bit == 0, ahead, behind)
        value = jnp.where(row_bit == chunk_bit, value, other)
    return value


def fold(value):
    total = jnp.sum(value.reshape(value.shape[0] // ROWS, ROWS, value.shape[1]), axis=0)
    parts = [total[:, i : i + LANES] for i in range(0, total.shape[1], LANES)]
    return functools.reduce(jnp.add, parts)


def shifted(field, prev_lon, next_lon, prev_lat, next_lat, has_prev, has_next):
    rows, cols = field.shape
    row = lax.broadcasted_iota(jnp.int32, field.shape, 0)
    lane = lax.broadcasted_iota(jnp.int32, prev_lat.shape, 1)
    west = jnp.where(row == 0, prev_lon[ROWS - 1 : ROWS, :], pltpu.roll(field, 1, 0))
    east = jnp.where(row == rows - 1, next_lon[0:1, :], pltpu.roll(field, rows - 1, 0))
    south = pltpu.roll(field, 1, 1)
    north = pltpu.roll(field, cols - 1, 1)
    first = jnp.where(lane == 0, pltpu.roll(prev_lat, 1, 1) * has_prev, south[:, :LANES])
    last = jnp.where(
        lane == LANES - 1, pltpu.roll(next_lat, LANES - 1, 1) * has_next, north[:, cols - LANES :]
    )
    south = jnp.concatenate([first, south[:, LANES:]], 1)
    north = jnp.concatenate([north[:, : cols - LANES], last], 1)
    return west + east + south + north


def kernel(
    n_lon,
    n_lat,
    kappa_ref,
    prior_ref,
    templates_hbm,
    count_ref,
    lon_ref,
    lat_ref,
    ids_ref,
    readings_ref,
    noise_ref,
    x_ref,
    r_ref,
    templates_ref,
    select_ref,
    columns_ref,
    padded_ref,
    placed_ref,
    spread_ref,
    patch_ref,
    ids_rows_ref,
    weights_ref,
    term_ref,
    p_ref,
    s_ref,
    u_ref,
    edge_lon,
    edge_lat,
    sum_a,
    sum_b,
    template_sem,
    edge_send,
    edge_recv,
    a_send,
    a_recv,
    b_send,
    b_recv,
):
    kinds, reads, cells = templates_ref.shape
    rows, cols = kappa_ref.shape
    blocks = ids_ref.shape[1]
    tiles = blocks // PER_TILE
    lon, lat = lax.axis_index("lon"), lax.axis_index("lat")
    group_a, group_b = 2 * n_lat, n_lon // 2
    core, me_b = lon % 2, lon // 2
    me_a = lat * 2 + core

    def peer_a(step):
        index = (me_a + step) % group_a
        return (me_b * 2 + index % 2, index // 2)

    def peer_b(step):
        return (((me_b + step) % group_b) * 2 + core, lat)

    lon_next, lon_prev = ((lon + 1) % n_lon, lat), ((lon + n_lon - 1) % n_lon, lat)
    lat_next, lat_prev = (lon, (lat + 1) % n_lat), (lon, (lat + n_lat - 1) % n_lat)

    template_copy = pltpu.make_async_copy(templates_hbm, templates_ref, template_sem)
    template_copy.start()

    barrier = pltpu.get_barrier_semaphore()
    peers = [lon_next, lon_prev, lat_next, lat_prev]
    peers += [peer_a(step) for step in range(1, group_a)]
    peers += [peer_b(step) for step in range(1, group_b)]
    for peer in peers:
        pl.semaphore_signal(barrier, inc=1, device_id=peer, device_id_type=MESH)

    def edges(source, kind, turn):
        pieces = [
            (source.at[pl.ds(rows - ROWS, ROWS), :], edge_lon.at[kind, turn, 0], lon_next),
            (source.at[pl.ds(0, ROWS), :], edge_lon.at[kind, turn, 1], lon_prev),
            (source.at[:, pl.ds(cols - LANES, LANES)], edge_lat.at[kind, turn, 0], lat_next),
            (source.at[:, pl.ds(0, LANES)], edge_lat.at[kind, turn, 1], lat_prev),
        ]
        return [
            pltpu.make_async_remote_copy(
                src_ref=src,
                dst_ref=dst,
                send_sem=edge_send.at[kind, turn, place],
                recv_sem=edge_recv.at[kind, turn, place],
                device_id=peer,
                device_id_type=MESH,
            )
            for place, (src, dst, peer) in enumerate(pieces)
        ]

    def sums(buffer, me, send, recv, turn, peers):
        return [
            pltpu.make_async_remote_copy(
                src_ref=buffer.at[turn, me],
                dst_ref=buffer.at[turn, me],
                send_sem=send.at[turn, step],
                recv_sem=recv.at[turn, step],
                device_id=peer,
                device_id_type=MESH,
            )
            for step, peer in enumerate(peers)
        ]

    has_prev = (lat > 0).astype(F32)
    has_next = (lat < n_lat - 1).astype(F32)

    def neighbours(field, kind, turn):
        return shifted(
            field,
            edge_lon[kind, turn, 0],
            edge_lon[kind, turn, 1],
            edge_lat[kind, turn, 0],
            edge_lat[kind, turn, 1],
            has_prev,
            has_next,
        )

    offset = lax.broadcasted_iota(jnp.int32, (PSIDE, cols), 1) - lax.broadcasted_iota(
        jnp.int32, (PSIDE, cols), 0
    )

    def one_selector(block, carry):
        start = pl.multiple_of(block * PSIDE, PSIDE)
        chosen = jnp.where(offset == lat_ref[0, block], 1.0, 0.0)
        select_ref[pl.ds(start, PSIDE), :] = chosen.astype(BF16)
        return carry

    lax.fori_loop(0, blocks, one_selector, 0)
    padded_ref[...] = jnp.zeros(padded_ref.shape, F32)
    p_ref[...] = jnp.zeros(p_ref.shape, F32)
    s_ref[...] = jnp.zeros(s_ref.shape, F32)
    x_ref[...] = jnp.zeros(x_ref.shape, F32)
    slot = lax.broadcasted_iota(jnp.int32, (blocks, reads), 0)
    weights_ref[...] = jnp.where(slot < count_ref[0], noise_ref[...], 0.0)
    ids_row = jnp.broadcast_to(ids_ref[...].astype(F32), (blocks, blocks))
    ids_rows_ref[...] = jnp.transpose(ids_row)
    chunk = lax.broadcasted_iota(jnp.int32, (ROWS, LANES), 1) // PSIDE

    def read(field):
        high, low = split(field)
        both = lax.dot_general(
            jnp.concatenate([high, low], 0), select_ref[...], NT, preferred_element_type=F32
        )
        both = both[:rows] + both[rows:]
        for tile in range(tiles):
            columns_ref[tile] = both[:, tile * LANES : (tile + 1) * LANES]

        def one_tile(tile, carry):
            halves = []
            for half in range(2):
                picked = jnp.zeros((ROWS, LANES), F32)
                for place in range(PER_TILE):
                    start = lon_ref[0, tile * PER_TILE + place] + half * ROWS
                    window = columns_ref[tile, pl.ds(start, ROWS), :]
                    picked = jnp.where(chunk == place, window, picked)
                halves.append(picked)
            turned = block_transpose(jnp.stack(halves))
            start = pl.multiple_of(tile * ROWS, ROWS)
            patch_ref[pl.ds(start, ROWS), 0:LANES] = turned[0]
            patch_ref[pl.ds(start, ROWS), LANES : 2 * LANES] = turned[1]
            return carry

        lax.fori_loop(0, tiles, one_tile, 0)
        high, low = split(jnp.transpose(patch_ref[...]))
        patches = jnp.concatenate([high, low], 1)
        ids = jnp.broadcast_to(ids_ref[...], (ROWS, blocks))
        some = 8

        def some_kinds(turn, acc):
            first = turn * some
            table = templates_ref[pl.ds(first, some)].reshape(some * reads, cells)
            result = jnp.dot(table, patches, preferred_element_type=F32)
            result = result[:, :blocks] + result[:, blocks:]
            for kind in range(some):
                mine = (ids == first + kind)[:1]
                acc = jnp.where(mine, result[kind * reads : (kind + 1) * reads], acc)
            return acc

        acc = lax.fori_loop(0, kinds // some, some_kinds, jnp.zeros((reads, blocks), F32))
        return jnp.transpose(acc)

    def spread(mixed):
        high, low = split(mixed)
        both = jnp.concatenate([high, low], 0)
        ids = ids_rows_ref[...].astype(BF16)
        ids = jnp.concatenate([ids, ids], 0)
        for kind in range(kinds):
            placed_ref[:, kind * reads : (kind + 1) * reads] = jnp.where(
                ids == kind, both, jnp.zeros_like(both)
            )
        terms = jnp.dot(
            placed_ref[...],
            templates_ref[...].reshape(kinds * reads, cells),
            preferred_element_type=F32,
        )
        terms = terms[:blocks] + terms[blocks:]
        lead = rows - PSIDE
        for half in range(2):
            part = terms[:, half * LANES : (half + 1) * LANES].reshape(tiles, ROWS, LANES)
            padded_ref[:, lead + half * ROWS : lead + (half + 1) * ROWS, :] = block_transpose(part)

        def one_tile(tile, carry):
            picked = jnp.zeros((rows, LANES), F32)
            wide = lax.broadcasted_iota(jnp.int32, (rows, LANES), 1) // PSIDE
            for place in range(PER_TILE):
                start = lead - lon_ref[0, tile * PER_TILE + place]
                window = padded_ref[tile, pl.ds(start, rows), :]
                picked = jnp.where(wide == place, window, picked)
            high, low = split(picked)
            start = pl.multiple_of(tile * LANES, LANES)
            spread_ref[0:rows, pl.ds(start, LANES)] = high
            spread_ref[rows : 2 * rows, pl.ds(start, LANES)] = low
            return carry

        lax.fori_loop(0, tiles, one_tile, 0)
        both = jnp.dot(spread_ref[...], select_ref[...], preferred_element_type=F32)
        return both[:rows] + both[rows:]

    template_copy.wait()
    r_ref[...] = spread(weights_ref[...] * readings_ref[...])
    pl.semaphore_wait(barrier, len(peers))

    def one_turn(turn, carry):
        norm_old, alpha_old = carry
        r_copies = edges(r_ref, 0, turn)
        for copy in r_copies:
            copy.start()
        residual = r_ref[...]
        image = read(residual)
        mixed = weights_ref[...] * image
        term_ref[...] = mixed
        for copy in r_copies:
            copy.wait_recv()
        first = (kappa_ref[...] + 4.0) * residual - neighbours(residual, 0, turn)
        scaled = prior_ref[...] * first
        u_ref[...] = scaled
        u_copies = edges(u_ref, 1, turn)
        for copy in u_copies:
            copy.start()
        sum_a[turn, me_a, 0:ROWS] = fold(residual * residual)
        sum_a[turn, me_a, ROWS : 2 * ROWS] = fold(scaled * first) + fold(mixed * image)
        a_copies = sums(
            sum_a, me_a, a_send, a_recv, turn, [peer_a(step) for step in range(1, group_a)]
        )
        for copy in a_copies:
            copy.start()
        observed = spread(term_ref[...])
        for copy in a_copies:
            copy.wait_recv()
        sum_b[turn, me_b] = jnp.sum(sum_a[turn], axis=0)
        b_copies = sums(
            sum_b, me_b, b_send, b_recv, turn, [peer_b(step) for step in range(1, group_b)]
        )
        for copy in b_copies:
            copy.start()
        for copy in u_copies:
            copy.wait_recv()
        scaled = u_ref[...]
        w = (kappa_ref[...] + 4.0) * scaled - neighbours(scaled, 1, turn) + observed
        for copy in b_copies:
            copy.wait_recv()
        total = jnp.sum(sum_b[turn], axis=0)
        norm = jnp.sum(total[:ROWS], keepdims=True)
        curve = jnp.sum(total[ROWS:], keepdims=True)
        beta = jnp.where(turn > 0, norm / norm_old, 0.0)
        alpha = norm / (curve - beta * norm / alpha_old)
        for copy in r_copies + u_copies + a_copies + b_copies:
            copy.wait_send()
        p = r_ref[...] + beta * p_ref[...]
        s = w + beta * s_ref[...]
        p_ref[...] = p
        s_ref[...] = s
        x_ref[...] += alpha * p
        r_ref[...] -= alpha * s
        return norm, alpha

    one = jnp.ones((1, 1), F32)
    lax.fori_loop(0, ITERS, one_turn, (one, one))


def on_device(
    n_lon,
    n_lat,
    kappa_sq,
    prior_scale,
    templates,
    block_counts,
    anchor_lon,
    anchor_lat,
    template_ids,
    readings,
    noise_prec,
):
    rows, cols = kappa_sq.shape
    kinds, reads, cells = templates.shape
    blocks = template_ids.shape[1]
    tiles = blocks // PER_TILE
    group_a, group_b = 2 * n_lat, n_lon // 2
    vmem = pl.BlockSpec(memory_space=pltpu.VMEM)
    smem = pl.BlockSpec(memory_space=pltpu.SMEM)
    dma = pltpu.SemaphoreType.DMA
    field = jax.ShapeDtypeStruct((rows, cols), F32)
    return pl.pallas_call(
        functools.partial(kernel, n_lon, n_lat),
        out_shape=(field, field),
        in_specs=[
            vmem,
            vmem,
            pl.BlockSpec(memory_space=pl.ANY),
            smem,
            smem,
            smem,
            vmem,
            vmem,
            vmem,
        ],
        out_specs=(vmem, vmem),
        scratch_shapes=[
            pltpu.VMEM((kinds, reads, cells), BF16),
            pltpu.VMEM((blocks * PSIDE, cols), BF16),
            pltpu.VMEM((tiles, rows, LANES), F32),
            pltpu.VMEM((tiles, 2 * rows - PSIDE, LANES), F32),
            pltpu.VMEM((2 * blocks, kinds * reads), BF16),
            pltpu.VMEM((2 * rows, blocks * PSIDE), BF16),
            pltpu.VMEM((blocks, cells), F32),
            pltpu.VMEM((blocks, blocks), F32),
            pltpu.VMEM((blocks, reads), F32),
            pltpu.VMEM((blocks, reads), F32),
            pltpu.VMEM((rows, cols), F32),
            pltpu.VMEM((rows, cols), F32),
            pltpu.VMEM((rows, cols), F32),
            pltpu.VMEM((2, ITERS, 2, ROWS, cols), F32),
            pltpu.VMEM((2, ITERS, 2, rows, LANES), F32),
            pltpu.VMEM((ITERS, group_a, 2 * ROWS, LANES), F32),
            pltpu.VMEM((ITERS, group_b, 2 * ROWS, LANES), F32),
            dma,
            dma((2, ITERS, 4)),
            dma((2, ITERS, 4)),
            dma((ITERS, group_a - 1)),
            dma((ITERS, group_a - 1)),
            dma((ITERS, group_b - 1)),
            dma((ITERS, group_b - 1)),
        ],
        compiler_params=pltpu.CompilerParams(
            collective_id=0, has_side_effects=True, vmem_limit_bytes=48 * 1024 * 1024
        ),
    )(
        kappa_sq,
        prior_scale,
        templates,
        block_counts,
        anchor_lon,
        anchor_lat,
        template_ids,
        readings[0],
        noise_prec[0],
    )


def solution(mesh):
    return jax.shard_map(
        functools.partial(on_device, mesh.shape["lon"], mesh.shape["lat"]),
        mesh=mesh,
        in_specs=(
            P("lon", "lat"),
            P("lon", "lat"),
            P(),
            P(("lon", "lat")),
            P("lon", "lat"),
            P("lon", "lat"),
            P("lon", "lat"),
            P("lon", "lat", None),
            P("lon", "lat", None),
        ),
        out_specs=(P("lon", "lat"), P("lon", "lat")),
        check_vma=False,
    )
```

time: 730 us -> 72.4 us (0.10); the launches traced: 722 us -> 72 us
  blocking collectives: 314 us -> 0 us
  matrix products: 166 us -> 0 us
  starting transfers between devices: 110 us -> 0 us
  Pallas kernels: 0 us -> 61.8 us
  waiting for transfers between devices: 60.2 us -> 0 us
  local copies, waits for them, and re-layouts: 38.5 us -> 8.94 us
  other arithmetic: 12.9 us -> 0 us
  loops' own time: 10.8 us -> 0 us
  between operations: 9.79 us -> 1.3 us
    psum x5 -> x0, blocking collectives: 314 us -> none  [the longest x3 188 us: squares(): return lax.psum(jnp.sum(vector * vector), ('lon', 'lat'))]
    dot_general x48 -> x0, matrix products: 166 us -> none  [the longest x8 57 us: one_group(): jnp.einsum('gri,gi->gr', chosen, patch, precision=lax.Precision.HIGHEST)]
    all_to_all x10 -> x0, starting transfers between devices: 66.9 us -> none  [the longest x3 21.7 us: on_device(): lax.all_to_all(observe_sent, ('lon', 'lat'), split_axis=0, concat_axis=0,...]
    pallas_call x0 -> x1, Pallas kernels: none -> 61.8 us  [on_device(): pl.pallas_call(functools.partial(kernel, n_lon, n_lat), out_shape=(field,...]
    all_to_all x10 -> x0, waiting for transfers between devices: 60.1 us -> none  [the longest x4 34.5 us: returned(): lax.all_to_all(sent, ('lon', 'lat'), split_axis=0, concat_axis=0, tiled=T...]
    ppermute x24 -> x0, starting transfers between devices: 42.8 us -> none  [the longest x12 29.8 us: extended(): lax.ppermute(tail, axis, [(i, (i + 1) % count) for i in range(ends)])]
    while x8 -> x0, local copies, waits for them, and re-layouts: 20 us -> none
    another operation x4 -> x0, loops' own time: 10.8 us -> none  [block_terms(): lax.fori_loop(0, turns, one_group, jnp.zeros(patches.shape, jnp.float32))]
  transfers between devices with their start and end apart: 34 -> 0, of which waited for: 9 -> 0; matrix products, arithmetic and copies ran while one was open for 19% -> 0% of each run, Pallas kernels for 0% -> 0%
where the time goes in v1:
time: 72.4 us; the launch traced here: 72 us
  Pallas kernels  61.8 us (85%)
  local copies, waits for them, and re-layouts  8.94 us (12%)
  between operations  1.3 us (2%)
    pallas_call x1, Pallas kernels, on_device(): pl.pallas_call(functools.partial(kernel, n_lon, n_lat), out_shape=(field,...  61.8 us
    unnamed x18, local copies, waits for them, and re-layouts  8.94 us

profile of v1, /device:TPU:1, one launch (start us, length us, event | category | flops | bytes accessed | tf_op | source)
XLA Modules:
  0.0 72.0 jit_solution(14042222186038059721)
XLA Ops:
  1.3 0.0 copy-start
  1.3 2.2 %copy-done = bf16[64,128,256]{2,1,0:T(8,128)(2,1)S(1)} copy-done((bf16[64,128,256]{2,1,0:T(8,128)(2,1)S(1)}, bf16[64,128,256]{2,1,0:T(8,128)(2,1)}, u32[]{:S(2)}) %copy-start) | copy-done | bytes 4194328
  3.5 0.0 copy-start.1
  3.5 0.9 %copy-done.1 = f32[64,512]{1,0:T(8,128)S(1)} copy-done((f32[64,512]{1,0:T(8,128)S(1)}, f32[64,512]{1,0:T(8,128)}, u32[]{:S(2)}) %copy-start.1) | copy-done | bytes 131096
  4.4 0.0 copy-start.2
  4.4 0.9 %copy-done.2 = f32[64,512]{1,0:T(8,128)S(1)} copy-done((f32[64,512]{1,0:T(8,128)S(1)}, f32[64,512]{1,0:T(8,128)}, u32[]{:S(2)}) %copy-start.2) | copy-done | bytes 131096
  5.3 0.0 copy-start.3
  5.3 0.8 %copy-done.3 = f32[1,128,128]{2,1,0:T(8,128)S(1)} copy-done((f32[1,128,128]{2,1,0:T(8,128)S(1)}, f32[1,128,128]{2,1,0:T(8,128)}, u32[]{:S(2)}) %copy-start.3) | copy-done | bytes 65560
  6.1 0.0 copy-start.4
  6.1 0.8 %copy-done.4 = f32[1,128,128]{2,1,0:T(8,128)S(1)} copy-done((f32[1,128,128]{2,1,0:T(8,128)S(1)}, f32[1,128,128]{2,1,0:T(8,128)}, u32[]{:S(2)}) %copy-start.4) | copy-done | bytes 65560
  7.0 0.0 copy-start.5
  7.0 0.7 copy-done.5
  7.6 0.0 copy-start.6
  7.6 0.7 copy-done.6
  8.3 0.0 copy-start.7
  8.3 0.7 copy-done.7
  8.9 61.8 %shard_map.104 = (f32[64,512]{1,0:T(8,128)S(1)}, f32[64,512]{1,0:T(8,128)S(1)}) custom-call(f32[64,512]{1,0:T(8,128)S(1)} %copy-done.1, f32[64,512]{1,0:T(8,128)S(1)} %copy-done.2, bf16[64,128,256]{2,1,0:T(8,128)(2,1)S(1)} %copy-done, s32[1]{0:T(128)S(6)} %copy.13.count_ref, s32[1,128]{1,0:T(1,128)S(1)} %copy-done.5, s32[1,128]{1,0:T(1,128)S(1)} %copy-done.6, ...), custom_call_target="tpu_custom_call" | custom-call | tf_op jit(solution)/shard_map/pallas_call | solution.py:365
  70.7 0.7 copy.14
  71.4 0.7 copy.15
Async XLA Ops:
  1.3 2.2 %copy-start = (bf16[64,128,256]{2,1,0:T(8,128)(2,1)S(1)}, bf16[64,128,256]{2,1,0:T(8,128)(2,1)}, u32[]{:S(2)}) copy-start(bf16[64,128,256]{2,1,0:T(8,128)(2,1)} %templates_hbm.1) | copy-start | bytes 12582916
  3.5 0.9 %copy-start.1 = (f32[64,512]{1,0:T(8,128)S(1)}, f32[64,512]{1,0:T(8,128)}, u32[]{:S(2)}) copy-start(f32[64,512]{1,0:T(8,128)} %kappa_ref.1) | copy-start | bytes 393220
  4.4 0.9 %copy-start.2 = (f32[64,512]{1,0:T(8,128)S(1)}, f32[64,512]{1,0:T(8,128)}, u32[]{:S(2)}) copy-start(f32[64,512]{1,0:T(8,128)} %prior_ref.1) | copy-start | bytes 393220
  5.3 0.8 %copy-start.3 = (f32[1,128,128]{2,1,0:T(8,128)S(1)}, f32[1,128,128]{2,1,0:T(8,128)}, u32[]{:S(2)}) copy-start(f32[1,128,128]{2,1,0:T(8,128)} %param.16) | copy-start | bytes 196612
  6.1 0.8 %copy-start.4 = (f32[1,128,128]{2,1,0:T(8,128)S(1)}, f32[1,128,128]{2,1,0:T(8,128)}, u32[]{:S(2)}) copy-start(f32[1,128,128]{2,1,0:T(8,128)} %param.17) | copy-start | bytes 196612
  7.0 0.7 copy-start.5
  7.6 0.7 copy-start.6
  8.3 0.7 copy-start.7

commit v2 on v1

v2 whole, which is shorter than its diff:
```python
import functools

import jax
import jax.numpy as jnp
from jax import lax
from jax.experimental import pallas as pl
from jax.experimental.pallas import tpu as pltpu
from jax.sharding import PartitionSpec as P

PSIDE = 16
ITERS = 3
LANES = 128
ROWS = 8
PER_TILE = LANES // PSIDE
F32 = jnp.float32
BF16 = jnp.bfloat16
MESH = pl.DeviceIdType.MESH


def split(value):
    high = value.astype(BF16)
    low = (value - high.astype(F32)).astype(BF16)
    return high, low


def block_transpose(value):
    row = lax.broadcasted_iota(jnp.int32, value.shape, 1)
    chunk = lax.broadcasted_iota(jnp.int32, value.shape, 2) // PSIDE
    for k in (4, 2, 1):
        row_bit = (row // k) % 2
        chunk_bit = (chunk // k) % 2
        ahead = pltpu.roll(pltpu.roll(value, ROWS - k, 1), PSIDE * k, 2)
        if k == 4:
            other = ahead
        else:
            behind = pltpu.roll(pltpu.roll(value, k, 1), LANES - PSIDE * k, 2)
            other = jnp.where(row_bit == 0, ahead, behind)
        value = jnp.where(row_bit == chunk_bit, value, other)
    return value


def fold(value):
    total = jnp.sum(value.reshape(value.shape[0] // ROWS, ROWS, value.shape[1]), axis=0)
    parts = [total[:, i : i + LANES] for i in range(0, total.shape[1], LANES)]
    return functools.reduce(jnp.add, parts)


def shifted(field, prev_lon, next_lon, prev_lat, next_lat, has_prev, has_next):
    rows, cols = field.shape
    row = lax.broadcasted_iota(jnp.int32, field.shape, 0)
    lane = lax.broadcasted_iota(jnp.int32, prev_lat.shape, 1)
    west = jnp.where(row == 0, prev_lon[ROWS - 1 : ROWS, :], pltpu.roll(field, 1, 0))
    east = jnp.where(row == rows - 1, next_lon[0:1, :], pltpu.roll(field, rows - 1, 0))
    south = pltpu.roll(field, 1, 1)
    north = pltpu.roll(field, cols - 1, 1)
    first = jnp.where(lane == 0, pltpu.roll(prev_lat, 1, 1) * has_prev, south[:, :LANES])
    last = jnp.where(
        lane == LANES - 1, pltpu.roll(next_lat, LANES - 1, 1) * has_next, north[:, cols - LANES :]
    )
    south = jnp.concatenate([first, south[:, LANES:]], 1)
    north = jnp.concatenate([north[:, : cols - LANES], last], 1)
    return west + east + south + north


def kernel(
    n_lon,
    n_lat,
    kappa_hbm,
    prior_hbm,
    templates_hbm,
    count_hbm,
    lon_hbm,
    lat_hbm,
    ids_hbm,
    readings_hbm,
    noise_hbm,
    x_ref,
    r_ref,
    kappa_ref,
    prior_ref,
    templates_ref,
    count_ref,
    lon_ref,
    lat_ref,
    ids_ref,
    readings_ref,
    weights_ref,
    select_ref,
    turned_ref,
    columns_ref,
    padded_ref,
    spread_ref,
    patch_ref,
    ids_rows_ref,
    term_ref,
    r0_ref,
    w0_ref,
    r1_ref,
    w1_ref,
    v_ref,
    u_ref,
    first_ref,
    edge_lon,
    edge_lat,
    first_a,
    first_b,
    last_a,
    last_b,
    load_sem,
    edge_send,
    edge_recv,
    first_a_send,
    first_a_recv,
    first_b_send,
    first_b_recv,
    last_a_send,
    last_a_recv,
    last_b_send,
    last_b_recv,
):
    kinds, reads, cells = templates_ref.shape
    rows, cols = kappa_ref.shape
    blocks = ids_ref.shape[1]
    tiles = blocks // PER_TILE
    lon, lat = lax.axis_index("lon"), lax.axis_index("lat")
    chips_lon = n_lon // 2
    core, chip = lon % 2, lon // 2

    loads = [
        pltpu.make_async_copy(source, target, load_sem.at[place])
        for place, (source, target) in enumerate(
            [
                (lat_hbm, lat_ref),
                (lon_hbm, lon_ref),
                (ids_hbm, ids_ref),
                (count_hbm, count_ref),
                (noise_hbm, weights_ref),
                (readings_hbm, readings_ref),
                (templates_hbm, templates_ref),
                (kappa_hbm, kappa_ref),
                (prior_hbm, prior_ref),
            ]
        )
    ]
    for copy in loads:
        copy.start()

    me_a = lat * 2 + core
    group_a = 2 * n_lat

    def peer_a(step):
        index = (me_a + step) % group_a
        return (chip * 2 + index % 2, index // 2)

    peers_a = [peer_a(step) for step in range(1, group_a)]
    peers_b = [(((chip + step) % chips_lon) * 2 + core, lat) for step in range(1, chips_lon)]
    twin = (chip * 2 + 1 - core, lat)
    peers_far = [
        (((chip + along) % chips_lon) * 2 + core, (lat + across) % n_lat)
        for across, along in far_first(n_lat, chips_lon)
    ]
    lon_next, lon_prev = ((lon + 1) % n_lon, lat), ((lon + n_lon - 1) % n_lon, lat)
    lat_next, lat_prev = (lon, (lat + 1) % n_lat), (lon, (lat + n_lat - 1) % n_lat)

    barrier = pltpu.get_barrier_semaphore()
    peers = [lon_next, lon_prev, lat_next, lat_prev, twin] + peers_a + peers_b + peers_far
    for peer in peers:
        pl.semaphore_signal(barrier, inc=1, device_id=peer, device_id_type=MESH)

    def edges(source, kind, turn):
        pieces = [
            (source.at[pl.ds(rows - ROWS, ROWS), :], edge_lon.at[kind, turn, 0], lon_next),
            (source.at[pl.ds(0, ROWS), :], edge_lon.at[kind, turn, 1], lon_prev),
            (source.at[:, pl.ds(cols - LANES, LANES)], edge_lat.at[kind, turn, 0], lat_next),
            (source.at[:, pl.ds(0, LANES)], edge_lat.at[kind, turn, 1], lat_prev),
        ]
        return [
            pltpu.make_async_remote_copy(
                src_ref=src,
                dst_ref=dst,
                send_sem=edge_send.at[kind, turn, place],
                recv_sem=edge_recv.at[kind, turn, place],
                device_id=peer,
                device_id_type=MESH,
            )
            for place, (src, dst, peer) in enumerate(pieces)
        ]

    def sums(buffer, me, send, recv, peers):
        return [
            pltpu.make_async_remote_copy(
                src_ref=buffer.at[me],
                dst_ref=buffer.at[me],
                send_sem=send.at[step],
                recv_sem=recv.at[step],
                device_id=peer,
                device_id_type=MESH,
            )
            for step, peer in enumerate(peers)
        ]

    first_a_copies = sums(first_a, me_a, first_a_send, first_a_recv, peers_a)
    first_b_copies = sums(first_b, chip, first_b_send, first_b_recv, peers_b)
    last_a_copies = sums(last_a, core, last_a_send, last_a_recv, [twin])
    me_far = chip * n_lat + lat
    last_b_copies = sums(last_b, me_far, last_b_send, last_b_recv, peers_far)

    has_prev = (lat > 0).astype(F32)
    has_next = (lat < n_lat - 1).astype(F32)

    def neighbours(field, kind, turn):
        return shifted(
            field,
            edge_lon[kind, turn, 0],
            edge_lon[kind, turn, 1],
            edge_lat[kind, turn, 0],
            edge_lat[kind, turn, 1],
            has_prev,
            has_next,
        )

    padded_ref[...] = jnp.zeros(padded_ref.shape, F32)
    offset = lax.broadcasted_iota(jnp.int32, (PSIDE, cols), 1) - lax.broadcasted_iota(
        jnp.int32, (PSIDE, cols), 0
    )

    def one_selector(block, carry):
        start = pl.multiple_of(block * PSIDE, PSIDE)
        chosen = jnp.where(offset == lat_ref[0, block], 1.0, 0.0)
        select_ref[pl.ds(start, PSIDE), :] = chosen.astype(BF16)
        return carry

    loads[0].wait()
    lax.fori_loop(0, blocks, one_selector, 0, unroll=16)
    lane = lax.broadcasted_iota(jnp.int32, (ROWS, LANES), 1)
    chunk = lane // PSIDE
    cell = lax.broadcasted_iota(jnp.int32, (cols, LANES), 0)

    def one_turned(tile, carry):
        place = jnp.zeros((ROWS, LANES), jnp.int32)
        for block in range(PER_TILE):
            place = jnp.where(chunk == block, lat_ref[0, tile * PER_TILE + block], place)
        place = (place + lane % PSIDE)[:1]
        start = pl.multiple_of(tile * LANES, LANES)
        turned_ref[:, pl.ds(start, LANES)] = jnp.where(cell == place, 1.0, 0.0).astype(BF16)
        return carry

    lax.fori_loop(0, tiles, one_turned, 0, unroll=2)
    for copy in loads[1:6]:
        copy.wait()
    slot = lax.broadcasted_iota(jnp.int32, (blocks, reads), 0)
    weights = jnp.where(slot < count_ref[0], weights_ref[...], 0.0)
    weights_ref[...] = weights
    term_ref[...] = weights * readings_ref[...]
    ids_row = jnp.broadcast_to(ids_ref[...].astype(F32), (blocks, blocks))
    ids_rows_ref[...] = jnp.transpose(ids_row)

    def gather(field):
        high, low = split(field)
        both = jnp.dot(
            jnp.concatenate([high, low], 0), turned_ref[...], preferred_element_type=F32
        )
        both = both[:rows] + both[rows:]
        for tile in range(tiles):
            columns_ref[tile] = both[:, tile * LANES : (tile + 1) * LANES]
        for tile in range(tiles):
            halves = []
            for half in range(2):
                picked = jnp.zeros((ROWS, LANES), F32)
                for place in range(PER_TILE):
                    start = lon_ref[0, tile * PER_TILE + place] + half * ROWS
                    window = columns_ref[tile, pl.ds(start, ROWS), :]
                    picked = jnp.where(chunk == place, window, picked)
                halves.append(picked)
            done = block_transpose(jnp.stack(halves))
            for half in range(2):
                patch_ref[
                    tile * ROWS : (tile + 1) * ROWS, half * LANES : (half + 1) * LANES
                ] = done[half]

    def read():
        high, low = split(jnp.transpose(patch_ref[...]))
        patches = jnp.concatenate([high, low], 1)
        ids = jnp.broadcast_to(ids_ref[...], (ROWS, blocks))
        ids = jnp.concatenate([ids, ids], 1)
        acc = jnp.zeros((reads, 2 * blocks), F32)
        for kind in range(kinds):
            result = jnp.dot(templates_ref[kind], patches, preferred_element_type=F32)
            acc = jnp.where((ids == kind)[:1], result, acc)
        return jnp.transpose(acc[:, :blocks] + acc[:, blocks:])

    def spread(mixed):
        high, low = split(mixed)
        both = jnp.concatenate([high, low], 0)
        ids = ids_rows_ref[...].astype(BF16)
        ids = jnp.concatenate([ids, ids], 0)
        terms = jnp.zeros((2 * blocks, cells), F32)
        some = 8
        for first in range(0, kinds, some):
            left = [
                jnp.where(ids == kind, both, jnp.zeros_like(both))
                for kind in range(first, first + some)
            ]
            table = templates_ref[first : first + some].reshape(some * reads, cells)
            terms += jnp.dot(jnp.concatenate(left, 1), table, preferred_element_type=F32)
        terms = terms[:blocks] + terms[blocks:]
        lead = rows - PSIDE
        for half in range(2):
            part = terms[:, half * LANES : (half + 1) * LANES].reshape(tiles, ROWS, LANES)
            padded_ref[:, lead + half * ROWS : lead + (half + 1) * ROWS, :] = block_transpose(part)
        wide = lax.broadcasted_iota(jnp.int32, (rows, LANES), 1) // PSIDE

        def one_tile(tile, carry):
            picked = jnp.zeros((rows, LANES), F32)
            for place in range(PER_TILE):
                start = lead - lon_ref[0, tile * PER_TILE + place]
                window = padded_ref[tile, pl.ds(start, rows), :]
                picked = jnp.where(wide == place, window, picked)
            high, low = split(picked)
            start = pl.multiple_of(tile * LANES, LANES)
            spread_ref[0:rows, pl.ds(start, LANES)] = high
            spread_ref[rows : 2 * rows, pl.ds(start, LANES)] = low
            return carry

        lax.fori_loop(0, tiles, one_tile, 0, unroll=4)
        both = jnp.dot(spread_ref[...], select_ref[...], preferred_element_type=F32)
        return both[:rows] + both[rows:]

    row_at = lax.broadcasted_iota(jnp.int32, (ROWS, LANES), 0)

    def packed(parts):
        parts = [jnp.sum(part, axis=0, keepdims=True) for part in parts]
        parts += [jnp.zeros((1, LANES), F32)] * (ROWS - len(parts))
        total = jnp.sum(jnp.concatenate(parts, 0), axis=1, keepdims=True)
        return jnp.sum(jnp.where(row_at == lane, total, 0.0), axis=0, keepdims=True)

    def unpacked(total, count):
        return [
            jnp.sum(jnp.where(lane[:1] == place, total, 0.0), axis=1, keepdims=True)
            for place in range(count)
        ]

    for copy in loads[6:]:
        copy.wait()
    right = spread(term_ref[...])
    r0_ref[...] = right
    v_ref[...] = right
    pl.semaphore_wait(barrier, len(peers))

    def one_turn(turn, carry):
        v_copies = edges(v_ref, 0, turn)
        for copy in v_copies:
            copy.start()
        gather(v_ref[...])

        @pl.when(turn == 1)
        def _():
            for copy in first_a_copies:
                copy.wait_recv()
            first_b[chip] = jnp.sum(first_a[...], axis=0)
            for copy in first_b_copies:
                copy.start()

        image = read()
        mixed = weights_ref[...] * image
        term_ref[...] = mixed
        for copy in v_copies:
            copy.wait_recv()
        field = v_ref[...]
        inner = (kappa_ref[...] + 4.0) * field - neighbours(field, 0, turn)
        scaled = prior_ref[...] * inner
        u_ref[...] = scaled
        u_copies = edges(u_ref, 1, turn)
        for copy in u_copies:
            copy.start()
        curve = fold(scaled * inner) + fold(mixed * image)

        @pl.when(turn == 0)
        def _():
            first_a[me_a] = packed([fold(r0_ref[...] * r0_ref[...]), curve])
            for copy in first_a_copies:
                copy.start()

        @pl.when(turn == 2)
        def _():
            r0, w0, r1, w1 = r0_ref[...], w0_ref[...], r1_ref[...], w1_ref[...]
            pairs = [(r0, r1), (r1, r1), (r1, w1), (r0, w1), (w0, w1), (w1, w1)]
            last_a[core] = packed([fold(one * two) for one, two in pairs] + [curve])
            for copy in last_a_copies:
                copy.start()
            for copy in last_a_copies:
                copy.wait_recv()
            last_b[me_far] = jnp.sum(last_a[...], axis=0)
            for copy in last_b_copies:
                copy.start()

        observed = spread(term_ref[...])
        for copy in u_copies:
            copy.wait_recv()
        scaled = u_ref[...]
        image = (kappa_ref[...] + 4.0) * scaled - neighbours(scaled, 1, turn) + observed
        for copy in v_copies + u_copies:
            copy.wait_send()

        @pl.when(turn == 0)
        def _():
            w0_ref[...] = image
            v_ref[...] = image

        @pl.when(turn == 1)
        def _():
            for copy in first_b_copies:
                copy.wait_recv()
            norm, curve = unpacked(jnp.sum(first_b[...], axis=0), 2)
            alpha = norm / curve
            w0 = w0_ref[...]
            w1 = w0 - alpha * image
            r1_ref[...] = r0_ref[...] - alpha * w0
            w1_ref[...] = w1
            v_ref[...] = w1
            lane_row = lane[:1]
            first_ref[...] = jnp.where(lane_row == 0, alpha, jnp.where(lane_row == 1, curve, 0.0))

        @pl.when(turn == 2)
        def _():
            for copy in last_b_copies:
                copy.wait_recv()
            sizes = unpacked(jnp.sum(last_b[...], axis=0), 7)
            alpha, a = unpacked(first_ref[...], 2)
            g0, g1, d, b, c, e, f = sizes
            g2 = d
            l1, l2 = b / a, c / a
            d, e, f = d - l1 * b, e - l1 * c, f - l2 * c
            m = e / d
            f = f - m * e
            g1 = g1 - l1 * g0
            g2 = g2 - l2 * g0 - m * g1
            c2 = g2 / f
            c1 = g1 / d - m * c2
            c0 = g0 / a - l1 * c1 - l2 * c2
            w1, r1 = w1_ref[...], r1_ref[...]
            x_ref[...] = (alpha + c0) * r0_ref[...] + c1 * r1 + c2 * w1
            r_ref[...] = r1 - c0 * w0_ref[...] - c1 * w1 - c2 * image

        return carry

    lax.fori_loop(0, ITERS, one_turn, 0)
    for copy in first_a_copies + first_b_copies + last_a_copies + last_b_copies:
        copy.wait_send()


def far_first(n_lat, chips_lon):
    side = max(1, round(chips_lon**0.5))

    def away(step, size):
        return min(step, size - step)

    steps = [
        (across, along)
        for across in range(n_lat)
        for along in range(chips_lon)
        if across or along
    ]

    def distance(step):
        across, along = step
        return away(across, n_lat) + away(along // side, side) + away(along % side, side)

    return sorted(steps, key=distance, reverse=True)


def on_device(
    n_lon,
    n_lat,
    kappa_sq,
    prior_scale,
    templates,
    block_counts,
    anchor_lon,
    anchor_lat,
    template_ids,
    readings,
    noise_prec,
):
    rows, cols = kappa_sq.shape
    kinds, reads, cells = templates.shape
    blocks = template_ids.shape[1]
    tiles = blocks // PER_TILE
    group_a, chips_lon = 2 * n_lat, n_lon // 2
    chips = n_lat * chips_lon
    vmem = pl.BlockSpec(memory_space=pltpu.VMEM)
    dma = pltpu.SemaphoreType.DMA
    field = jax.ShapeDtypeStruct((rows, cols), F32)
    plane = pltpu.VMEM((rows, cols), F32)
    return pl.pallas_call(
        functools.partial(kernel, n_lon, n_lat),
        out_shape=(field, field),
        in_specs=[pl.BlockSpec(memory_space=pl.ANY)] * 9,
        out_specs=(vmem, vmem),
        scratch_shapes=[
            plane,
            plane,
            pltpu.VMEM((kinds, reads, cells), BF16),
            pltpu.SMEM((1,), jnp.int32),
            pltpu.SMEM((1, blocks), jnp.int32),
            pltpu.SMEM((1, blocks), jnp.int32),
            pltpu.VMEM((1, blocks), jnp.int32),
            pltpu.VMEM((blocks, reads), F32),
            pltpu.VMEM((blocks, reads), F32),
            pltpu.VMEM((blocks * PSIDE, cols), BF16),
            pltpu.VMEM((cols, blocks * PSIDE), BF16),
            pltpu.VMEM((tiles, rows, LANES), F32),
            pltpu.VMEM((tiles, 2 * rows - PSIDE, LANES), F32),
            pltpu.VMEM((2 * rows, blocks * PSIDE), BF16),
            pltpu.VMEM((blocks, cells), F32),
            pltpu.VMEM((blocks, blocks), F32),
            pltpu.VMEM((blocks, reads), F32),
            plane,
            plane,
            plane,
            plane,
            plane,
            plane,
            pltpu.VMEM((1, LANES), F32),
            pltpu.VMEM((2, ITERS, 2, ROWS, cols), F32),
            pltpu.VMEM((2, ITERS, 2, rows, LANES), F32),
            pltpu.VMEM((group_a, 1, LANES), F32),
            pltpu.VMEM((chips_lon, 1, LANES), F32),
            pltpu.VMEM((2, 1, LANES), F32),
            pltpu.VMEM((chips, 1, LANES), F32),
            dma((9,)),
            dma((2, ITERS, 4)),
            dma((2, ITERS, 4)),
            dma((group_a - 1,)),
            dma((group_a - 1,)),
            dma((chips_lon - 1,)),
            dma((chips_lon - 1,)),
            dma((1,)),
            dma((1,)),
            dma((chips - 1,)),
            dma((chips - 1,)),
        ],
        compiler_params=pltpu.CompilerParams(
            collective_id=0, has_side_effects=True, vmem_limit_bytes=60 * 1024 * 1024
        ),
    )(
        kappa_sq,
        prior_scale,
        templates,
        block_counts,
        anchor_lon,
        anchor_lat,
        template_ids,
        readings[0],
        noise_prec[0],
    )


def solution(mesh):
    return jax.shard_map(
        functools.partial(on_device, mesh.shape["lon"], mesh.shape["lat"]),
        mesh=mesh,
        in_specs=(
            P("lon", "lat"),
            P("lon", "lat"),
            P(),
            P(("lon", "lat")),
            P("lon", "lat"),
            P("lon", "lat"),
            P("lon", "lat"),
            P("lon", "lat", None),
            P("lon", "lat", None),
        ),
        out_specs=(P("lon", "lat"), P("lon", "lat")),
        check_vma=False,
    )
```

time: 72.4 us -> 44.9 us (0.62)
  Pallas kernels: 61.8 us -> 39.9 us
  local copies, waits for them, and re-layouts: 8.94 us -> 3.14 us
    pallas_call x1, Pallas kernels: 61.8 us -> 39.9 us  [on_device(): pl.pallas_call(functools.partial(kernel, n_lon, n_lat), out_shape=(field,...]
    unnamed x18 -> x2, local copies, waits for them, and re-layouts: 8.94 us -> 3.14 us
where the time goes in v2:
time: 44.9 us; the launch traced here: 44.3 us
  Pallas kernels  39.9 us (89%)
  local copies, waits for them, and re-layouts  3.14 us (7%)
  between operations  1.29 us (3%)
    pallas_call x1, Pallas kernels, on_device(): pl.pallas_call(functools.partial(kernel, n_lon, n_lat), out_shape=(field,...  39.9 us
    unnamed x2, local copies, waits for them, and re-layouts  3.14 us

profile of v2, /device:TPU:1, one launch (start us, length us, event | category | flops | bytes accessed | tf_op | source)
XLA Modules:
  0.0 44.3 jit_solution(17634588956253057064)
XLA Ops:
  1.3 39.9 %shard_map.104 = (f32[64,512]{1,0:T(8,128)}, f32[64,512]{1,0:T(8,128)}) custom-call(f32[64,512]{1,0:T(8,128)} %kappa_hbm.1, f32[64,512]{1,0:T(8,128)} %prior_hbm.1, bf16[64,128,256]{2,1,0:T(8,128)(2,1)} %templates_hbm.1, s32[1]{0:T(128)S(6)} %copy.13.count_hbm, s32[1,128]{1,0:T(1,128)} %lon_hbm.1, s32[1,128]{1,0:T(1,128)} %lat_hbm.1, s32[1,128]{1,0:T(1,128)} %ids_hbm.1, ...), custom_call_target="tpu_custom_call" | custom-call | tf_op jit(solution)/shard_map/pallas_call | solution.py:495
  41.2 1.6 %copy.14 = f32[64,512]{1,0:T(8,128)} copy(f32[64,512]{1,0:T(8,128)} %get-tuple-element.4) | data formatting | bytes 262144
  42.8 1.6 %copy.15 = f32[64,512]{1,0:T(8,128)} copy(f32[64,512]{1,0:T(8,128)} %get-tuple-element.5) | data formatting | bytes 262144

commit v3 on v2

--- a/solution.py
+++ b/solution.py
@@ -9,6 +9,7 @@
 
 PSIDE = 16
 ITERS = 3
+TEMPLATE_PARTS = 8
 LANES = 128
 ROWS = 8
 PER_TILE = LANES // PSIDE
@@ -97,6 +98,7 @@
     w0_ref,
     r1_ref,
     w1_ref,
+    image_ref,
     v_ref,
     u_ref,
     first_ref,
@@ -126,6 +128,7 @@
     chips_lon = n_lon // 2
     core, chip = lon % 2, lon // 2
 
+    part = kinds // TEMPLATE_PARTS
     loads = [
         pltpu.make_async_copy(source, target, load_sem.at[place])
         for place, (source, target) in enumerate(
@@ -136,7 +139,12 @@
                 (count_hbm, count_ref),
                 (noise_hbm, weights_ref),
                 (readings_hbm, readings_ref),
-                (templates_hbm, templates_ref),
+            ]
+            + [
+                (templates_hbm.at[pl.ds(i * part, part)], templates_ref.at[pl.ds(i * part, part)])
+                for i in range(TEMPLATE_PARTS)
+            ]
+            + [
                 (kappa_hbm, kappa_ref),
                 (prior_hbm, prior_ref),
             ]
@@ -163,7 +171,7 @@
     lat_next, lat_prev = (lon, (lat + 1) % n_lat), (lon, (lat + n_lat - 1) % n_lat)
 
     barrier = pltpu.get_barrier_semaphore()
-    peers = [lon_next, lon_prev, lat_next, lat_prev, twin] + peers_a + peers_b + peers_far
+    peers = [lon_next, lon_prev, lat_next, lat_prev] + peers_a + peers_b
     for peer in peers:
         pl.semaphore_signal(barrier, inc=1, device_id=peer, device_id_type=MESH)
 
@@ -322,7 +330,7 @@
             spread_ref[rows : 2 * rows, pl.ds(start, LANES)] = low
             return carry
 
-        lax.fori_loop(0, tiles, one_tile, 0, unroll=4)
+        lax.fori_loop(0, tiles, one_tile, 0, unroll=tiles)
         both = jnp.dot(spread_ref[...], select_ref[...], preferred_element_type=F32)
         return both[:rows] + both[rows:]
 
@@ -342,86 +350,49 @@
 
     for copy in loads[6:]:
         copy.wait()
-    right = spread(term_ref[...])
-    r0_ref[...] = right
-    v_ref[...] = right
-    pl.semaphore_wait(barrier, len(peers))
 
     def one_turn(turn, carry):
-        v_copies = edges(v_ref, 0, turn)
-        for copy in v_copies:
-            copy.start()
-        gather(v_ref[...])
+        image_ref[...] = spread(term_ref[...])
+
+        @pl.when(turn > 0)
+        def _():
+            v_copies, u_copies = edges(v_ref, 0, turn - 1), edges(u_ref, 1, turn - 1)
+            for copy in u_copies:
+                copy.wait_recv()
+            scaled = u_ref[...]
+            around = neighbours(scaled, 1, turn - 1)
+            image_ref[...] += (kappa_ref[...] + 4.0) * scaled - around
+            for copy in v_copies + u_copies:
+                copy.wait_send()
+
+        @pl.when(turn == 0)
+        def _():
+            right = image_ref[...]
+            r0_ref[...] = right
+            v_ref[...] = right
+            pl.semaphore_wait(barrier, len(peers))
 
         @pl.when(turn == 1)
         def _():
-            for copy in first_a_copies:
-                copy.wait_recv()
-            first_b[chip] = jnp.sum(first_a[...], axis=0)
-            for copy in first_b_copies:
-                copy.start()
-
-        image = read()
-        mixed = weights_ref[...] * image
-        term_ref[...] = mixed
-        for copy in v_copies:
-            copy.wait_recv()
-        field = v_ref[...]
-        inner = (kappa_ref[...] + 4.0) * field - neighbours(field, 0, turn)
-        scaled = prior_ref[...] * inner
-        u_ref[...] = scaled
-        u_copies = edges(u_ref, 1, turn)
-        for copy in u_copies:
-            copy.start()
-        curve = fold(scaled * inner) + fold(mixed * image)
-
-        @pl.when(turn == 0)
-        def _():
-            first_a[me_a] = packed([fold(r0_ref[...] * r0_ref[...]), curve])
-            for copy in first_a_copies:
-                copy.start()
-
-        @pl.when(turn == 2)
-        def _():
-            r0, w0, r1, w1 = r0_ref[...], w0_ref[...], r1_ref[...], w1_ref[...]
-            pairs = [(r0, r1), (r1, r1), (r1, w1), (r0, w1), (w0, w1), (w1, w1)]
-            last_a[core] = packed([fold(one * two) for one, two in pairs] + [curve])
-            for copy in last_a_copies:
-                copy.start()
-            for copy in last_a_copies:
-                copy.wait_recv()
-            last_b[me_far] = jnp.sum(last_a[...], axis=0)
-            for copy in last_b_copies:
-                copy.start()
-
-        observed = spread(term_ref[...])
-        for copy in u_copies:
-            copy.wait_recv()
-        scaled = u_ref[...]
-        image = (kappa_ref[...] + 4.0) * scaled - neighbours(scaled, 1, turn) + observed
-        for copy in v_copies + u_copies:
-            copy.wait_send()
-
-        @pl.when(turn == 0)
-        def _():
+            image = image_ref[...]
             w0_ref[...] = image
             v_ref[...] = image
 
-        @pl.when(turn == 1)
+        @pl.when(turn == 2)
         def _():
             for copy in first_b_copies:
                 copy.wait_recv()
             norm, curve = unpacked(jnp.sum(first_b[...], axis=0), 2)
             alpha = norm / curve
             w0 = w0_ref[...]
-            w1 = w0 - alpha * image
+            w1 = w0 - alpha * image_ref[...]
             r1_ref[...] = r0_ref[...] - alpha * w0
             w1_ref[...] = w1
             v_ref[...] = w1
             lane_row = lane[:1]
             first_ref[...] = jnp.where(lane_row == 0, alpha, jnp.where(lane_row == 1, curve, 0.0))
 
-        @pl.when(turn == 2)
+        @pl.when(turn == ITERS)
         def _():
             for copy in last_b_copies:
                 copy.wait_recv()
@@ -440,11 +411,58 @@
             c0 = g0 / a - l1 * c1 - l2 * c2
             w1, r1 = w1_ref[...], r1_ref[...]
             x_ref[...] = (alpha + c0) * r0_ref[...] + c1 * r1 + c2 * w1
-            r_ref[...] = r1 - c0 * w0_ref[...] - c1 * w1 - c2 * image
+            r_ref[...] = r1 - c0 * w0_ref[...] - c1 * w1 - c2 * image_ref[...]
+
+        @pl.when(turn < ITERS)
+        def _():
+            v_copies, u_copies = edges(v_ref, 0, turn), edges(u_ref, 1, turn)
+            for copy in v_copies:
+                copy.start()
+            gather(v_ref[...])
+
+            @pl.when(turn == 1)
+            def _():
+                for copy in first_a_copies:
+                    copy.wait_recv()
+                first_b[chip] = jnp.sum(first_a[...], axis=0)
+                for copy in first_b_copies:
+                    copy.start()
+
+            image = read()
+            mixed = weights_ref[...] * image
+            term_ref[...] = mixed
+            for copy in v_copies:
+                copy.wait_recv()
+            field = v_ref[...]
+            inner = (kappa_ref[...] + 4.0) * field - neighbours(field, 0, turn)
+            scaled = prior_ref[...] * inner
+            u_ref[...] = scaled
+            for copy in u_copies:
+                copy.start()
+            curve = fold(scaled * inner) + fold(mixed * image)
+
+            @pl.when(turn == 0)
+            def _():
+                first_a[me_a] = packed([fold(r0_ref[...] * r0_ref[...]), curve])
+                for copy in first_a_copies:
+                    copy.start()
+
+            @pl.when(turn == 2)
+            def _():
+                r0, w0, r1, w1 = r0_ref[...], w0_ref[...], r1_ref[...], w1_ref[...]
+                pairs = [(r0, r1), (r1, r1), (r1, w1), (r0, w1), (w0, w1), (w1, w1)]
+                last_a[core] = packed([fold(one * two) for one, two in pairs] + [curve])
+                for copy in last_a_copies:
+                    copy.start()
+                for copy in last_a_copies:
+                    copy.wait_recv()
+                last_b[me_far] = jnp.sum(last_a[...], axis=0)
+                for copy in last_b_copies:
+                    copy.start()
 
         return carry
 
-    lax.fori_loop(0, ITERS, one_turn, 0)
+    lax.fori_loop(0, ITERS + 1, one_turn, 0)
     for copy in first_a_copies + first_b_copies + last_a_copies + last_b_copies:
         copy.wait_send()
 
@@ -467,6 +485,17 @@
         return away(across, n_lat) + away(along // side, side) + away(along % side, side)
 
     return sorted(steps, key=distance, reverse=True)
+
+
+def hand_out(x_in, r_in, x_out, r_out, sem):
+    copies = [
+        pltpu.make_async_copy(x_in, x_out, sem.at[0]),
+        pltpu.make_async_copy(r_in, r_out, sem.at[1]),
+    ]
+    for copy in copies:
+        copy.start()
+    for copy in copies:
+        copy.wait()
 
 
 def on_device(
@@ -492,9 +521,9 @@
     dma = pltpu.SemaphoreType.DMA
     field = jax.ShapeDtypeStruct((rows, cols), F32)
     plane = pltpu.VMEM((rows, cols), F32)
-    return pl.pallas_call(
+    fields = pl.pallas_call(
         functools.partial(kernel, n_lon, n_lat),
-        out_shape=(field, field),
+        out_shape=(pltpu.VMEM((rows, cols), F32), pltpu.VMEM((rows, cols), F32)),
         in_specs=[pl.BlockSpec(memory_space=pl.ANY)] * 9,
         out_specs=(vmem, vmem),
         scratch_shapes=[
@@ -521,6 +550,7 @@
             plane,
             plane,
             plane,
+            plane,
             pltpu.VMEM((1, LANES), F32),
             pltpu.VMEM((2, ITERS, 2, ROWS, cols), F32),
             pltpu.VMEM((2, ITERS, 2, rows, LANES), F32),
@@ -528,7 +558,7 @@
             pltpu.VMEM((chips_lon, 1, LANES), F32),
             pltpu.VMEM((2, 1, LANES), F32),
             pltpu.VMEM((chips, 1, LANES), F32),
-            dma((9,)),
+            dma((8 + TEMPLATE_PARTS,)),
             dma((2, ITERS, 4)),
             dma((2, ITERS, 4)),
             dma((group_a - 1,)),
@@ -541,7 +571,7 @@
             dma((chips - 1,)),
         ],
         compiler_params=pltpu.CompilerParams(
-            collective_id=0, has_side_effects=True, vmem_limit_bytes=60 * 1024 * 1024
+            collective_id=0, has_side_effects=True, vmem_limit_bytes=56 * 1024 * 1024
         ),
     )(
         kappa_sq,
@@ -554,6 +584,13 @@
         readings[0],
         noise_prec[0],
     )
+    return pl.pallas_call(
+        hand_out,
+        out_shape=(field, field),
+        in_specs=[vmem, vmem],
+        out_specs=(pl.BlockSpec(memory_space=pl.ANY),) * 2,
+        scratch_shapes=[dma((2,))],
+    )(*fields)
 
 
 def solution(mesh):

time: 44.9 us -> 43.3 us (0.964)
  local copies, waits for them, and re-layouts: 3.14 us -> 1.28 us
    unnamed x2 -> x4, local copies, waits for them, and re-layouts: 3.14 us -> 1.28 us
    pallas_call x1 -> x2, Pallas kernels: 39.9 us -> 40.2 us  [the longest x1 38.5 us: on_device(): pl.pallas_call(functools.partial(kernel, n_lon, n_lat), out_shape=(pltpu....]
where the time goes in v3:
time: 43.3 us; the launch traced here: 42.8 us
  Pallas kernels  40.2 us (93%)
  between operations  1.3 us (3%)
  local copies, waits for them, and re-layouts  1.28 us (3%)
    pallas_call x1, Pallas kernels, on_device(): pl.pallas_call(functools.partial(kernel, n_lon, n_lat), out_shape=(pltpu....  38.5 us
    pallas_call x1, Pallas kernels, on_device(): pl.pallas_call(hand_out, out_shape=(field, field), in_specs=[vmem, vmem],...  1.68 us
    unnamed x4, local copies, waits for them, and re-layouts  1.28 us

profile of v3, /device:TPU:1, one launch (start us, length us, event | category | flops | bytes accessed | tf_op | source)
XLA Modules:
  0.0 42.8 jit_solution(6035881363854034036)
XLA Ops:
  1.3 38.5 %shard_map.104 = (f32[64,512]{1,0:T(8,128)S(1)}, f32[64,512]{1,0:T(8,128)S(1)}) custom-call(f32[64,512]{1,0:T(8,128)} %kappa_hbm.1, f32[64,512]{1,0:T(8,128)} %prior_hbm.1, bf16[64,128,256]{2,1,0:T(8,128)(2,1)} %templates_hbm.1, s32[1]{0:T(128)S(6)} %copy.11.count_hbm, s32[1,128]{1,0:T(1,128)} %lon_hbm.1, s32[1,128]{1,0:T(1,128)} %lat_hbm.1, ...), custom_call_target="tpu_custom_call" | custom-call | tf_op jit(solution)/shard_map/pallas_call | solution.py:524
  39.8 0.0 copy-start
  39.8 0.6 %copy-done = f32[64,512]{1,0:T(8,128)} copy-done((f32[64,512]{1,0:T(8,128)}, f32[64,512]{1,0:T(8,128)S(1)}, u32[]{:S(2)}) %copy-start) | copy-done | bytes 131096
  40.5 0.0 copy-start.1
  40.5 0.6 %copy-done.1 = f32[64,512]{1,0:T(8,128)} copy-done((f32[64,512]{1,0:T(8,128)}, f32[64,512]{1,0:T(8,128)S(1)}, u32[]{:S(2)}) %copy-start.1) | copy-done | bytes 131096
  41.1 1.7 %shard_map.105 = (f32[64,512]{1,0:T(8,128)}, f32[64,512]{1,0:T(8,128)}) custom-call(f32[64,512]{1,0:T(8,128)} %copy-done, f32[64,512]{1,0:T(8,128)} %copy-done.1), custom_call_target="tpu_custom_call" | custom-call | tf_op jit(solution)/shard_map/pallas_call | solution.py:587
Async XLA Ops:
  39.8 0.6 %copy-start = (f32[64,512]{1,0:T(8,128)}, f32[64,512]{1,0:T(8,128)S(1)}, u32[]{:S(2)}) copy-start(f32[64,512]{1,0:T(8,128)S(1)} %get-tuple-element.4.x_in) | copy-start | bytes 393220
  40.5 0.6 %copy-start.1 = (f32[64,512]{1,0:T(8,128)}, f32[64,512]{1,0:T(8,128)S(1)}, u32[]{:S(2)}) copy-start(f32[64,512]{1,0:T(8,128)S(1)} %get-tuple-element.5.r_in) | copy-start | bytes 393220

commit v4 on v3

--- a/solution.py
+++ b/solution.py
@@ -46,18 +46,30 @@
     return functools.reduce(jnp.add, parts)
 
 
-def shifted(field, prev_lon, next_lon, prev_lat, next_lat, has_prev, has_next):
+def to_row(column):
+    wide = jnp.broadcast_to(column, (column.shape[0], LANES))
+    row = lax.broadcasted_iota(jnp.int32, wide.shape, 0)
+    lane = lax.broadcasted_iota(jnp.int32, wide.shape, 1)
+    return jnp.sum(jnp.where(row == lane, wide, 0.0), axis=0, keepdims=True)
+
+
+def to_column(row_value, rows):
+    wide = jnp.broadcast_to(row_value, (rows, LANES))
+    row = lax.broadcasted_iota(jnp.int32, wide.shape, 0)
+    lane = lax.broadcasted_iota(jnp.int32, wide.shape, 1)
+    return jnp.sum(jnp.where(row == lane, wide, 0.0), axis=1, keepdims=True)
+
+
+def shifted(field, prev_lon, next_lon, prev_lat, next_lat):
     rows, cols = field.shape
     row = lax.broadcasted_iota(jnp.int32, field.shape, 0)
-    lane = lax.broadcasted_iota(jnp.int32, prev_lat.shape, 1)
-    west = jnp.where(row == 0, prev_lon[ROWS - 1 : ROWS, :], pltpu.roll(field, 1, 0))
-    east = jnp.where(row == rows - 1, next_lon[0:1, :], pltpu.roll(field, rows - 1, 0))
+    lane = lax.broadcasted_iota(jnp.int32, (rows, LANES), 1)
+    west = jnp.where(row == 0, prev_lon, pltpu.roll(field, 1, 0))
+    east = jnp.where(row == rows - 1, next_lon, pltpu.roll(field, rows - 1, 0))
     south = pltpu.roll(field, 1, 1)
     north = pltpu.roll(field, cols - 1, 1)
-    first = jnp.where(lane == 0, pltpu.roll(prev_lat, 1, 1) * has_prev, south[:, :LANES])
-    last = jnp.where(
-        lane == LANES - 1, pltpu.roll(next_lat, LANES - 1, 1) * has_next, north[:, cols - LANES :]
-    )
+    first = jnp.where(lane == 0, prev_lat, south[:, :LANES])
+    last = jnp.where(lane == LANES - 1, next_lat, north[:, cols - LANES :])
     south = jnp.concatenate([first, south[:, LANES:]], 1)
     north = jnp.concatenate([north[:, : cols - LANES], last], 1)
     return west + east + south + north
@@ -102,8 +114,13 @@
     v_ref,
     u_ref,
     first_ref,
+    curve_ref,
+    out_lon,
+    out_lat,
+    out_corner,
     edge_lon,
     edge_lat,
+    edge_corner,
     first_a,
     first_b,
     last_a,
@@ -169,30 +186,58 @@
     ]
     lon_next, lon_prev = ((lon + 1) % n_lon, lat), ((lon + n_lon - 1) % n_lon, lat)
     lat_next, lat_prev = (lon, (lat + 1) % n_lat), (lon, (lat + n_lat - 1) % n_lat)
+    corners = [(one[0], two[1]) for one in (lon_next, lon_prev) for two in (lat_next, lat_prev)]
 
     barrier = pltpu.get_barrier_semaphore()
-    peers = [lon_next, lon_prev, lat_next, lat_prev] + peers_a + peers_b
+    peers = [lon_next, lon_prev, lat_next, lat_prev] + corners + peers_a + peers_b
     for peer in peers:
         pl.semaphore_signal(barrier, inc=1, device_id=peer, device_id_type=MESH)
 
-    def edges(source, kind, turn):
-        pieces = [
-            (source.at[pl.ds(rows - ROWS, ROWS), :], edge_lon.at[kind, turn, 0], lon_next),
-            (source.at[pl.ds(0, ROWS), :], edge_lon.at[kind, turn, 1], lon_prev),
-            (source.at[:, pl.ds(cols - LANES, LANES)], edge_lat.at[kind, turn, 0], lat_next),
-            (source.at[:, pl.ds(0, LANES)], edge_lat.at[kind, turn, 1], lat_prev),
+    def pack_vector(field):
+        out_lon[0, 0, 0] = field[rows - 1 : rows, :]
+        out_lon[0, 0, 1] = field[rows - 2 : rows - 1, :]
+        out_lon[0, 1, 0] = field[0:1, :]
+        out_lon[0, 1, 1] = field[1:2, :]
+        out_lat[0, 0, 0] = to_row(field[:, cols - 1 : cols])
+        out_lat[0, 0, 1] = to_row(field[:, cols - 2 : cols - 1])
+        out_lat[0, 1, 0] = to_row(field[:, 0:1])
+        out_lat[0, 1, 1] = to_row(field[:, 1:2])
+        for place, (row, col) in enumerate([(rows - 1, cols - 1), (rows - 1, 0), (0, cols - 1), (0, 0)]):
+            value = field[row : row + 1, col : col + 1]
+            out_corner[place] = jnp.broadcast_to(value, (1, LANES))
+
+    def pack_coefficients(kappa, prior):
+        for place, field in enumerate((kappa, prior)):
+            out_lon[1, 0, place] = field[rows - 1 : rows, :]
+            out_lon[1, 1, place] = field[0:1, :]
+            out_lat[1, 0, place] = to_row(field[:, cols - 1 : cols])
+            out_lat[1, 1, place] = to_row(field[:, 0:1])
+
+    def remote(src, dst, slot, place, peer):
+        return pltpu.make_async_remote_copy(
+            src_ref=src,
+            dst_ref=dst,
+            send_sem=edge_send.at[slot, place],
+            recv_sem=edge_recv.at[slot, place],
+            device_id=peer,
+            device_id_type=MESH,
+        )
+
+    def sides(kind, slot):
+        return [
+            remote(out_lon.at[kind, 0], edge_lon.at[slot, 0], slot, 0, lon_next),
+            remote(out_lon.at[kind, 1], edge_lon.at[slot, 1], slot, 1, lon_prev),
+            remote(out_lat.at[kind, 0], edge_lat.at[slot, 0], slot, 2, lat_next),
+            remote(out_lat.at[kind, 1], edge_lat.at[slot, 1], slot, 3, lat_prev),
         ]
+
+    def diagonals(slot):
         return [
-            pltpu.make_async_remote_copy(
-                src_ref=src,
-                dst_ref=dst,
-                send_sem=edge_send.at[kind, turn, place],
-                recv_sem=edge_recv.at[kind, turn, place],
-                device_id=peer,
-                device_id_type=MESH,
-            )
-            for place, (src, dst, peer) in enumerate(pieces)
+            remote(out_corner.at[place], edge_corner.at[slot, place], slot, 4 + place, peer)
+            for place, peer in enumerate(corners)
         ]
+
+    coefficient_copies = sides(1, ITERS)
 
     def sums(buffer, me, send, recv, peers):
         return [
@@ -216,16 +261,45 @@
     has_prev = (lat > 0).astype(F32)
     has_next = (lat < n_lat - 1).astype(F32)
 
-    def neighbours(field, kind, turn):
-        return shifted(
+    def inner_stencil(turn):
+        field = v_ref[...]
+        around = shifted(
             field,
-            edge_lon[kind, turn, 0],
-            edge_lon[kind, turn, 1],
-            edge_lat[kind, turn, 0],
-            edge_lat[kind, turn, 1],
-            has_prev,
-            has_next,
+            edge_lon[turn, 0, 0],
+            edge_lon[turn, 1, 0],
+            to_column(edge_lat[turn, 0, 0] * has_prev, rows),
+            to_column(edge_lat[turn, 1, 0] * has_next, rows),
         )
+        inner = (kappa_ref[...] + 4.0) * field - around
+        scaled = prior_ref[...] * inner
+        u_ref[...] = scaled
+        return inner, scaled
+
+    def outer_stencil(turn):
+        lane_wide = lax.broadcasted_iota(jnp.int32, (1, cols), 1)
+        lane_row = lax.broadcasted_iota(jnp.int32, (1, LANES), 1)
+        present = (has_prev, has_next)
+        beside_lon, beside_lat = [], []
+        for side, at in ((0, 0), (1, rows - 1)):
+            near, far = edge_lon[turn, side, 0], edge_lon[turn, side, 1]
+            kappa, prior = edge_lon[ITERS, side, 0], edge_lon[ITERS, side, 1]
+            first = edge_corner[turn, 2 * side][:, :1] * has_prev
+            last = edge_corner[turn, 2 * side + 1][:, :1] * has_next
+            south = jnp.where(lane_wide == 0, first, pltpu.roll(near, 1, 1))
+            north = jnp.where(lane_wide == cols - 1, last, pltpu.roll(near, cols - 1, 1))
+            around = far + v_ref[at : at + 1, :] + south + north
+            beside_lon.append(prior * ((kappa + 4.0) * near - around))
+        for side in (0, 1):
+            near, far = edge_lat[turn, side, 0], edge_lat[turn, side, 1]
+            kappa, prior = edge_lat[ITERS, side, 0], edge_lat[ITERS, side, 1]
+            first, last = edge_corner[turn, side][:, :1], edge_corner[turn, 2 + side][:, :1]
+            west = jnp.where(lane_row == 0, first, pltpu.roll(near, 1, 1))
+            east = jnp.where(lane_row == rows - 1, last, pltpu.roll(near, LANES - 1, 1))
+            around = far + out_lat[0, 1 - side, 0] + west + east
+            value = prior * ((kappa + 4.0) * near - around) * present[side]
+            beside_lat.append(to_column(value, rows))
+        scaled = u_ref[...]
+        return (kappa_ref[...] + 4.0) * scaled - shifted(scaled, *beside_lon, *beside_lat)
 
     padded_ref[...] = jnp.zeros(padded_ref.shape, F32)
     offset = lax.broadcasted_iota(jnp.int32, (PSIDE, cols), 1) - lax.broadcasted_iota(
@@ -350,19 +424,28 @@
 
     for copy in loads[6:]:
         copy.wait()
+    pack_coefficients(kappa_ref[...], prior_ref[...])
 
     def one_turn(turn, carry):
         image_ref[...] = spread(term_ref[...])
 
+        @pl.when(turn == 2)
+        def _():
+            for copy in sides(0, turn - 1):
+                copy.wait_recv()
+            inner_stencil(turn - 1)
+
+        @pl.when(turn == 1)
+        def _():
+            for copy in coefficient_copies:
+                copy.wait_recv()
+
         @pl.when(turn > 0)
         def _():
-            v_copies, u_copies = edges(v_ref, 0, turn - 1), edges(u_ref, 1, turn - 1)
-            for copy in u_copies:
+            for copy in diagonals(turn - 1):
                 copy.wait_recv()
-            scaled = u_ref[...]
-            around = neighbours(scaled, 1, turn - 1)
-            image_ref[...] += (kappa_ref[...] + 4.0) * scaled - around
-            for copy in v_copies + u_copies:
+            image_ref[...] += outer_stencil(turn - 1)
+            for copy in sides(0, turn - 1) + diagonals(turn - 1):
                 copy.wait_send()
 
         @pl.when(turn == 0)
@@ -415,9 +498,15 @@
 
         @pl.when(turn < ITERS)
         def _():
-            v_copies, u_copies = edges(v_ref, 0, turn), edges(u_ref, 1, turn)
-            for copy in v_copies:
+            pack_vector(v_ref[...])
+            for copy in sides(0, turn) + diagonals(turn):
                 copy.start()
+
+            @pl.when(turn == 0)
+            def _():
+                for copy in coefficient_copies:
+                    copy.start()
+
             gather(v_ref[...])
 
             @pl.when(turn == 1)
@@ -431,19 +520,17 @@
             image = read()
             mixed = weights_ref[...] * image
             term_ref[...] = mixed
-            for copy in v_copies:
-                copy.wait_recv()
-            field = v_ref[...]
-            inner = (kappa_ref[...] + 4.0) * field - neighbours(field, 0, turn)
-            scaled = prior_ref[...] * inner
-            u_ref[...] = scaled
-            for copy in u_copies:
-                copy.start()
-            curve = fold(scaled * inner) + fold(mixed * image)
+
+            @pl.when(turn != 1)
+            def _():
+                for copy in sides(0, turn):
+                    copy.wait_recv()
+                inner, scaled = inner_stencil(turn)
+                curve_ref[...] = fold(scaled * inner) + fold(mixed * image)
 
             @pl.when(turn == 0)
             def _():
-                first_a[me_a] = packed([fold(r0_ref[...] * r0_ref[...]), curve])
+                first_a[me_a] = packed([fold(r0_ref[...] * r0_ref[...]), curve_ref[...]])
                 for copy in first_a_copies:
                     copy.start()
 
@@ -451,7 +538,7 @@
             def _():
                 r0, w0, r1, w1 = r0_ref[...], w0_ref[...], r1_ref[...], w1_ref[...]
                 pairs = [(r0, r1), (r1, r1), (r1, w1), (r0, w1), (w0, w1), (w1, w1)]
-                last_a[core] = packed([fold(one * two) for one, two in pairs] + [curve])
+                last_a[core] = packed([fold(one * two) for one, two in pairs] + [curve_ref[...]])
                 for copy in last_a_copies:
                     copy.start()
                 for copy in last_a_copies:
@@ -463,7 +550,7 @@
         return carry
 
     lax.fori_loop(0, ITERS + 1, one_turn, 0)
-    for copy in first_a_copies + first_b_copies + last_a_copies + last_b_copies:
+    for copy in first_a_copies + first_b_copies + last_a_copies + last_b_copies + coefficient_copies:
         copy.wait_send()
 
 
@@ -552,15 +639,20 @@
             plane,
             plane,
             pltpu.VMEM((1, LANES), F32),
-            pltpu.VMEM((2, ITERS, 2, ROWS, cols), F32),
-            pltpu.VMEM((2, ITERS, 2, rows, LANES), F32),
+            pltpu.VMEM((ROWS, LANES), F32),
+            pltpu.VMEM((2, 2, 2, 1, cols), F32),
+            pltpu.VMEM((2, 2, 2, 1, LANES), F32),
+            pltpu.VMEM((4, 1, LANES), F32),
+            pltpu.VMEM((ITERS + 1, 2, 2, 1, cols), F32),
+            pltpu.VMEM((ITERS + 1, 2, 2, 1, LANES), F32),
+            pltpu.VMEM((ITERS, 4, 1, LANES), F32),
             pltpu.VMEM((group_a, 1, LANES), F32),
             pltpu.VMEM((chips_lon, 1, LANES), F32),
             pltpu.VMEM((2, 1, LANES), F32),
             pltpu.VMEM((chips, 1, LANES), F32),
             dma((8 + TEMPLATE_PARTS,)),
-            dma((2, ITERS, 4)),
-            dma((2, ITERS, 4)),
+            dma((ITERS + 1, 8)),
+            dma((ITERS + 1, 8)),
             dma((group_a - 1,)),
             dma((group_a - 1,)),
             dma((chips_lon - 1,)),
@@ -587,9 +679,10 @@
     return pl.pallas_call(
         hand_out,
         out_shape=(field, field),
-        in_specs=[vmem, vmem],
+        in_specs=[pl.BlockSpec(memory_space=pl.ANY)] * 2,
         out_specs=(pl.BlockSpec(memory_space=pl.ANY),) * 2,
         scratch_shapes=[dma((2,))],
+        compiler_params=pltpu.CompilerParams(vmem_limit_bytes=1024 * 1024),
     )(*fields)
 
 

time: 43.3 us -> 38.4 us (0.89)
  Pallas kernels: 40.2 us -> 36.5 us
  local copies, waits for them, and re-layouts: 1.28 us -> 0 us
    pallas_call x1, Pallas kernels: 38.5 us -> 35.8 us  [on_device(): pl.pallas_call(functools.partial(kernel, n_lon, n_lat), out_shape=(pltpu....]
    unnamed x4 -> x0, local copies, waits for them, and re-layouts: 1.28 us -> none
    pallas_call x1, Pallas kernels: 1.68 us -> 0.72 us  [on_device(): pl.pallas_call(hand_out, out_shape=(field, field), in_specs=[pl.BlockSpec...]
where the time goes in v4:
time: 38.4 us; the launch traced here: 37.8 us
  Pallas kernels  36.5 us (95%)
  between operations  1.29 us (3%)
    pallas_call x1, Pallas kernels, on_device(): pl.pallas_call(functools.partial(kernel, n_lon, n_lat), out_shape=(pltpu....  35.8 us

profile of v4, /device:TPU:1, one launch (start us, length us, event | category | flops | bytes accessed | tf_op | source)
XLA Modules:
  0.0 37.8 jit_solution(5749739610300536706)
XLA Ops:
  1.3 35.8 %shard_map.104 = (f32[64,512]{1,0:T(8,128)S(1)}, f32[64,512]{1,0:T(8,128)S(1)}) custom-call(f32[64,512]{1,0:T(8,128)} %kappa_hbm.1, f32[64,512]{1,0:T(8,128)} %prior_hbm.1, bf16[64,128,256]{2,1,0:T(8,128)(2,1)} %templates_hbm.1, s32[1]{0:T(128)S(6)} %copy.11.count_hbm, s32[1,128]{1,0:T(1,128)} %lon_hbm.1, s32[1,128]{1,0:T(1,128)} %lat_hbm.1, ...), custom_call_target="tpu_custom_call" | custom-call | tf_op jit(solution)/shard_map/pallas_call | solution.py:611
  37.1 0.7 %shard_map.105 = (f32[64,512]{1,0:T(8,128)}, f32[64,512]{1,0:T(8,128)}) custom-call(f32[64,512]{1,0:T(8,128)S(1)} %get-tuple-element.4.x_in, f32[64,512]{1,0:T(8,128)S(1)} %get-tuple-element.5.r_in), custom_call_target="tpu_custom_call" | custom-call | tf_op jit(solution)/shard_map/pallas_call | solution.py:679

commit v5 on v4

--- a/solution.py
+++ b/solution.py
@@ -9,7 +9,6 @@
 
 PSIDE = 16
 ITERS = 3
-TEMPLATE_PARTS = 8
 LANES = 128
 ROWS = 8
 PER_TILE = LANES // PSIDE
@@ -128,14 +127,11 @@
     load_sem,
     edge_send,
     edge_recv,
-    first_a_send,
-    first_a_recv,
-    first_b_send,
-    first_b_recv,
-    last_a_send,
-    last_a_recv,
-    last_b_send,
-    last_b_recv,
+    corner_sem,
+    first_a_sem,
+    first_b_sem,
+    last_a_sem,
+    last_b_sem,
 ):
     kinds, reads, cells = templates_ref.shape
     rows, cols = kappa_ref.shape
@@ -145,23 +141,17 @@
     chips_lon = n_lon // 2
     core, chip = lon % 2, lon // 2
 
-    part = kinds // TEMPLATE_PARTS
     loads = [
         pltpu.make_async_copy(source, target, load_sem.at[place])
         for place, (source, target) in enumerate(
             [
                 (lat_hbm, lat_ref),
+                (templates_hbm, templates_ref),
                 (lon_hbm, lon_ref),
                 (ids_hbm, ids_ref),
                 (count_hbm, count_ref),
                 (noise_hbm, weights_ref),
                 (readings_hbm, readings_ref),
-            ]
-            + [
-                (templates_hbm.at[pl.ds(i * part, part)], templates_ref.at[pl.ds(i * part, part)])
-                for i in range(TEMPLATE_PARTS)
-            ]
-            + [
                 (kappa_hbm, kappa_ref),
                 (prior_hbm, prior_ref),
             ]
@@ -213,51 +203,68 @@
             out_lat[1, 0, place] = to_row(field[:, cols - 1 : cols])
             out_lat[1, 1, place] = to_row(field[:, 0:1])
 
-    def remote(src, dst, slot, place, peer):
+    def remote(src, dst, send_sem, recv_sem, peer):
         return pltpu.make_async_remote_copy(
             src_ref=src,
             dst_ref=dst,
-            send_sem=edge_send.at[slot, place],
-            recv_sem=edge_recv.at[slot, place],
+            send_sem=send_sem,
+            recv_sem=recv_sem,
             device_id=peer,
             device_id_type=MESH,
         )
 
-    def sides(kind, slot):
-        return [
-            remote(out_lon.at[kind, 0], edge_lon.at[slot, 0], slot, 0, lon_next),
-            remote(out_lon.at[kind, 1], edge_lon.at[slot, 1], slot, 1, lon_prev),
-            remote(out_lat.at[kind, 0], edge_lat.at[slot, 0], slot, 2, lat_next),
-            remote(out_lat.at[kind, 1], edge_lat.at[slot, 1], slot, 3, lat_prev),
-        ]
-
-    def diagonals(slot):
-        return [
-            remote(out_corner.at[place], edge_corner.at[slot, place], slot, 4 + place, peer)
-            for place, peer in enumerate(corners)
-        ]
-
-    coefficient_copies = sides(1, ITERS)
-
-    def sums(buffer, me, send, recv, peers):
-        return [
-            pltpu.make_async_remote_copy(
-                src_ref=buffer.at[me],
-                dst_ref=buffer.at[me],
-                send_sem=send.at[step],
-                recv_sem=recv.at[step],
-                device_id=peer,
-                device_id_type=MESH,
-            )
-            for step, peer in enumerate(peers)
-        ]
-
-    first_a_copies = sums(first_a, me_a, first_a_send, first_a_recv, peers_a)
-    first_b_copies = sums(first_b, chip, first_b_send, first_b_recv, peers_b)
-    last_a_copies = sums(last_a, core, last_a_send, last_a_recv, [twin])
+    def whole(ref, sem):
+        pltpu.make_async_copy(ref, ref, sem).wait()
+
+    def send_sides(kind, slot):
+        for side, peer in enumerate((lon_next, lon_prev)):
+            remote(
+                out_lon.at[kind, side],
+                edge_lon.at[slot, side],
+                edge_send.at[kind, 0],
+                edge_recv.at[slot, 0],
+                peer,
+            ).start()
+        for side, peer in enumerate((lat_next, lat_prev)):
+            remote(
+                out_lat.at[kind, side],
+                edge_lat.at[slot, side],
+                edge_send.at[kind, 1],
+                edge_recv.at[slot, 1],
+                peer,
+            ).start()
+
+    def receive_sides(slot):
+        whole(edge_lon.at[slot], edge_recv.at[slot, 0])
+        whole(edge_lat.at[slot], edge_recv.at[slot, 1])
+
+    def finish_sides(kind):
+        whole(out_lon.at[kind], edge_send.at[kind, 0])
+        whole(out_lat.at[kind], edge_send.at[kind, 1])
+
+    def send_corners(slot):
+        for place, peer in enumerate(corners):
+            remote(
+                out_corner.at[place],
+                edge_corner.at[slot, place],
+                corner_sem.at[ITERS],
+                corner_sem.at[slot],
+                peer,
+            ).start()
+
+    def send_sum(buffer, me, sems, peers):
+        for peer in peers:
+            remote(buffer.at[me], buffer.at[me], sems.at[0], sems.at[1], peer).start()
+
+    def receive_sum(buffer, sems):
+        others = buffer.at[pl.ds(0, buffer.shape[0] - 1)]
+        whole(others, sems.at[1])
+        return jnp.sum(buffer[...], axis=0)
+
+    def finish_sum(buffer, sems):
+        whole(buffer.at[pl.ds(0, buffer.shape[0] - 1)], sems.at[0])
+
     me_far = chip * n_lat + lat
-    last_b_copies = sums(last_b, me_far, last_b_send, last_b_recv, peers_far)
-
     has_prev = (lat > 0).astype(F32)
     has_next = (lat < n_lat - 1).astype(F32)
 
@@ -270,10 +277,32 @@
             to_column(edge_lat[turn, 0, 0] * has_prev, rows),
             to_column(edge_lat[turn, 1, 0] * has_next, rows),
         )
+        u_ref[...] = prior_ref[...] * ((kappa_ref[...] + 4.0) * field - around)
+
+    def inner_square():
+        field = v_ref[...]
+        nothing = jnp.zeros((1, cols), F32), jnp.zeros((rows, 1), F32)
+        around = shifted(field, nothing[0], nothing[0], nothing[1], nothing[1])
         inner = (kappa_ref[...] + 4.0) * field - around
-        scaled = prior_ref[...] * inner
-        u_ref[...] = scaled
-        return inner, scaled
+        lon_sides = inner[0:1, :], inner[rows - 1 : rows, :]
+        lat_sides = to_row(inner[:, 0:1]), to_row(inner[:, cols - 1 : cols])
+        return fold(prior_ref[...] * inner * inner), lon_sides, lat_sides
+
+    def side_square(turn, lon_sides, lat_sides):
+        lane_row = lax.broadcasted_iota(jnp.int32, (1, LANES), 1)
+        total = jnp.zeros((1, LANES), F32)
+        for side in (0, 1):
+            beside, own = edge_lon[turn, side, 0], lon_sides[side]
+            change = out_lon[1, 1 - side, 1] * beside * (beside - 2.0 * own)
+            for at in range(0, cols, LANES):
+                total += change[:, at : at + LANES]
+        ends = edge_lon[turn, 0, 0], edge_lon[turn, 1, 0]
+        for side, (at, present) in enumerate(((0, has_prev), (cols - 1, has_next))):
+            beside, own = edge_lat[turn, side, 0] * present, lat_sides[side]
+            own = own - jnp.where(lane_row == 0, ends[0][:, at : at + 1], 0.0)
+            own = own - jnp.where(lane_row == rows - 1, ends[1][:, at : at + 1], 0.0)
+            total += out_lat[1, 1 - side, 1] * beside * (beside - 2.0 * own)
+        return total
 
     def outer_stencil(turn):
         lane_wide = lax.broadcasted_iota(jnp.int32, (1, cols), 1)
@@ -328,7 +357,7 @@
         return carry
 
     lax.fori_loop(0, tiles, one_turned, 0, unroll=2)
-    for copy in loads[1:6]:
+    for copy in loads[2:]:
         copy.wait()
     slot = lax.broadcasted_iota(jnp.int32, (blocks, reads), 0)
     weights = jnp.where(slot < count_ref[0], weights_ref[...], 0.0)
@@ -410,8 +439,9 @@
 
     row_at = lax.broadcasted_iota(jnp.int32, (ROWS, LANES), 0)
 
-    def packed(parts):
+    def packed(parts, more):
         parts = [jnp.sum(part, axis=0, keepdims=True) for part in parts]
+        parts[-1] = parts[-1] + more
         parts += [jnp.zeros((1, LANES), F32)] * (ROWS - len(parts))
         total = jnp.sum(jnp.concatenate(parts, 0), axis=1, keepdims=True)
         return jnp.sum(jnp.where(row_at == lane, total, 0.0), axis=0, keepdims=True)
@@ -422,31 +452,27 @@
             for place in range(count)
         ]
 
-    for copy in loads[6:]:
-        copy.wait()
     pack_coefficients(kappa_ref[...], prior_ref[...])
+    loads[1].wait()
 
     def one_turn(turn, carry):
         image_ref[...] = spread(term_ref[...])
 
+        @pl.when(turn == 1)
+        def _():
+            receive_sides(ITERS)
+
         @pl.when(turn == 2)
         def _():
-            for copy in sides(0, turn - 1):
-                copy.wait_recv()
-            inner_stencil(turn - 1)
-
-        @pl.when(turn == 1)
-        def _():
-            for copy in coefficient_copies:
-                copy.wait_recv()
+            receive_sides(turn - 1)
 
         @pl.when(turn > 0)
         def _():
-            for copy in diagonals(turn - 1):
-                copy.wait_recv()
+            inner_stencil(turn - 1)
+            whole(edge_corner.at[turn - 1], corner_sem.at[turn - 1])
             image_ref[...] += outer_stencil(turn - 1)
-            for copy in sides(0, turn - 1) + diagonals(turn - 1):
-                copy.wait_send()
+            finish_sides(0)
+            whole(out_corner, corner_sem.at[ITERS])
 
         @pl.when(turn == 0)
         def _():
@@ -463,9 +489,7 @@
 
         @pl.when(turn == 2)
         def _():
-            for copy in first_b_copies:
-                copy.wait_recv()
-            norm, curve = unpacked(jnp.sum(first_b[...], axis=0), 2)
+            norm, curve = unpacked(receive_sum(first_b, first_b_sem), 2)
             alpha = norm / curve
             w0 = w0_ref[...]
             w1 = w0 - alpha * image_ref[...]
@@ -477,9 +501,7 @@
 
         @pl.when(turn == ITERS)
         def _():
-            for copy in last_b_copies:
-                copy.wait_recv()
-            sizes = unpacked(jnp.sum(last_b[...], axis=0), 7)
+            sizes = unpacked(receive_sum(last_b, last_b_sem), 7)
             alpha, a = unpacked(first_ref[...], 2)
             g0, g1, d, b, c, e, f = sizes
             g2 = d
@@ -499,59 +521,57 @@
         @pl.when(turn < ITERS)
         def _():
             pack_vector(v_ref[...])
-            for copy in sides(0, turn) + diagonals(turn):
-                copy.start()
+            send_sides(0, turn)
+            send_corners(turn)
 
             @pl.when(turn == 0)
             def _():
-                for copy in coefficient_copies:
-                    copy.start()
+                send_sides(1, ITERS)
 
             gather(v_ref[...])
 
             @pl.when(turn == 1)
             def _():
-                for copy in first_a_copies:
-                    copy.wait_recv()
-                first_b[chip] = jnp.sum(first_a[...], axis=0)
-                for copy in first_b_copies:
-                    copy.start()
+                first_b[chip] = receive_sum(first_a, first_a_sem)
+                send_sum(first_b, chip, first_b_sem, peers_b)
 
             image = read()
             mixed = weights_ref[...] * image
             term_ref[...] = mixed
-
-            @pl.when(turn != 1)
-            def _():
-                for copy in sides(0, turn):
-                    copy.wait_recv()
-                inner, scaled = inner_stencil(turn)
-                curve_ref[...] = fold(scaled * inner) + fold(mixed * image)
+            curve_ref[...] = fold(mixed * image)
+
+            def curve():
+                inside, lon_sides, lat_sides = inner_square()
+                return curve_ref[...] + inside, lon_sides, lat_sides
 
             @pl.when(turn == 0)
             def _():
-                first_a[me_a] = packed([fold(r0_ref[...] * r0_ref[...]), curve_ref[...]])
-                for copy in first_a_copies:
-                    copy.start()
+                inside, lon_sides, lat_sides = curve()
+                parts = [fold(r0_ref[...] * r0_ref[...]), inside]
+                receive_sides(turn)
+                first_a[me_a] = packed(parts, side_square(turn, lon_sides, lat_sides))
+                send_sum(first_a, me_a, first_a_sem, peers_a)
 
             @pl.when(turn == 2)
             def _():
                 r0, w0, r1, w1 = r0_ref[...], w0_ref[...], r1_ref[...], w1_ref[...]
                 pairs = [(r0, r1), (r1, r1), (r1, w1), (r0, w1), (w0, w1), (w1, w1)]
-                last_a[core] = packed([fold(one * two) for one, two in pairs] + [curve_ref[...]])
-                for copy in last_a_copies:
-                    copy.start()
-                for copy in last_a_copies:
-                    copy.wait_recv()
-                last_b[me_far] = jnp.sum(last_a[...], axis=0)
-                for copy in last_b_copies:
-                    copy.start()
+                inside, lon_sides, lat_sides = curve()
+                parts = [fold(one * two) for one, two in pairs] + [inside]
+                receive_sides(turn)
+                last_a[core] = packed(parts, side_square(turn, lon_sides, lat_sides))
+                send_sum(last_a, core, last_a_sem, [twin])
+                last_b[me_far] = receive_sum(last_a, last_a_sem)
+                send_sum(last_b, me_far, last_b_sem, peers_far)
 
         return carry
 
     lax.fori_loop(0, ITERS + 1, one_turn, 0)
-    for copy in first_a_copies + first_b_copies + last_a_copies + last_b_copies + coefficient_copies:
-        copy.wait_send()
+    finish_sides(1)
+    finish_sum(first_a, first_a_sem)
+    finish_sum(first_b, first_b_sem)
+    finish_sum(last_a, last_a_sem)
+    finish_sum(last_b, last_b_sem)
 
 
 def far_first(n_lat, chips_lon):
@@ -650,17 +670,14 @@
             pltpu.VMEM((chips_lon, 1, LANES), F32),
             pltpu.VMEM((2, 1, LANES), F32),
             pltpu.VMEM((chips, 1, LANES), F32),
-            dma((8 + TEMPLATE_PARTS,)),
-            dma((ITERS + 1, 8)),
-            dma((ITERS + 1, 8)),
-            dma((group_a - 1,)),
-            dma((group_a - 1,)),
-            dma((chips_lon - 1,)),
-            dma((chips_lon - 1,)),
-            dma((1,)),
-            dma((1,)),
-            dma((chips - 1,)),
-            dma((chips - 1,)),
+            dma((9,)),
+            dma((2, 2)),
+            dma((ITERS + 1, 2)),
+            dma((ITERS + 1,)),
+            dma((2,)),
+            dma((2,)),
+            dma((2,)),
+            dma((2,)),
         ],
         compiler_params=pltpu.CompilerParams(
             collective_id=0, has_side_effects=True, vmem_limit_bytes=56 * 1024 * 1024

time: 38.4 us -> 36.1 us (0.940)
  Pallas kernels: 36.5 us -> 34.2 us
    pallas_call x1, Pallas kernels: 35.8 us -> 33.5 us  [on_device(): pl.pallas_call(functools.partial(kernel, n_lon, n_lat), out_shape=(pltpu....]
where the time goes in v5:
time: 36.1 us; the launch traced here: 35.5 us
  Pallas kernels  34.2 us (95%)
  between operations  1.29 us (4%)
    pallas_call x1, Pallas kernels, on_device(): pl.pallas_call(functools.partial(kernel, n_lon, n_lat), out_shape=(pltpu....  33.5 us

profile of v5, /device:TPU:1, one launch (start us, length us, event | category | flops | bytes accessed | tf_op | source)
XLA Modules:
  0.0 35.5 jit_solution(1188856138570574370)
XLA Ops:
  1.3 33.5 %shard_map.104 = (f32[64,512]{1,0:T(8,128)S(1)}, f32[64,512]{1,0:T(8,128)S(1)}) custom-call(f32[64,512]{1,0:T(8,128)} %kappa_hbm.1, f32[64,512]{1,0:T(8,128)} %prior_hbm.1, bf16[64,128,256]{2,1,0:T(8,128)(2,1)} %templates_hbm.1, s32[1]{0:T(128)S(6)} %copy.11.count_hbm, s32[1,128]{1,0:T(1,128)} %lon_hbm.1, s32[1,128]{1,0:T(1,128)} %lat_hbm.1, ...), custom_call_target="tpu_custom_call" | custom-call | tf_op jit(solution)/shard_map/pallas_call | solution.py:631
  34.8 0.7 %shard_map.105 = (f32[64,512]{1,0:T(8,128)}, f32[64,512]{1,0:T(8,128)}) custom-call(f32[64,512]{1,0:T(8,128)S(1)} %get-tuple-element.4.x_in, f32[64,512]{1,0:T(8,128)S(1)} %get-tuple-element.5.r_in), custom_call_target="tpu_custom_call" | custom-call | tf_op jit(solution)/shard_map/pallas_call | solution.py:696

commit v6 on v5

--- a/solution.py
+++ b/solution.py
@@ -23,20 +23,24 @@
     return high, low
 
 
-def block_transpose(value):
+def slide(value):
+    chunk = lax.broadcasted_iota(jnp.int32, value.shape, 2) // PSIDE
+    for k in (1, 2, 4):
+        value = jnp.where((chunk // k) % 2 == 1, pltpu.roll(value, ROWS - k, 1), value)
+    return value
+
+
+def turn_blocks(value):
+    return slide(pltpu.roll(slide(value), 0, 2, stride=PSIDE, stride_axis=1))
+
+
+def negate_rows(value):
     row = lax.broadcasted_iota(jnp.int32, value.shape, 1)
-    chunk = lax.broadcasted_iota(jnp.int32, value.shape, 2) // PSIDE
-    for k in (4, 2, 1):
-        row_bit = (row // k) % 2
-        chunk_bit = (chunk // k) % 2
-        ahead = pltpu.roll(pltpu.roll(value, ROWS - k, 1), PSIDE * k, 2)
-        if k == 4:
-            other = ahead
-        else:
-            behind = pltpu.roll(pltpu.roll(value, k, 1), LANES - PSIDE * k, 2)
-            other = jnp.where(row_bit == 0, ahead, behind)
-        value = jnp.where(row_bit == chunk_bit, value, other)
-    return value
+    value = pltpu.roll(value, 4, 1)
+    for k in (2, 1):
+        ahead, behind = pltpu.roll(value, ROWS - k, 1), pltpu.roll(value, k, 1)
+        value = jnp.where((row // k) % 2 == 0, ahead, behind)
+    return pltpu.roll(value, 1, 1)
 
 
 def fold(value):
@@ -183,18 +187,24 @@
     for peer in peers:
         pl.semaphore_signal(barrier, inc=1, device_id=peer, device_id_type=MESH)
 
-    def pack_vector(field):
-        out_lon[0, 0, 0] = field[rows - 1 : rows, :]
-        out_lon[0, 0, 1] = field[rows - 2 : rows - 1, :]
-        out_lon[0, 1, 0] = field[0:1, :]
-        out_lon[0, 1, 1] = field[1:2, :]
-        out_lat[0, 0, 0] = to_row(field[:, cols - 1 : cols])
-        out_lat[0, 0, 1] = to_row(field[:, cols - 2 : cols - 1])
-        out_lat[0, 1, 0] = to_row(field[:, 0:1])
-        out_lat[0, 1, 1] = to_row(field[:, 1:2])
-        for place, (row, col) in enumerate([(rows - 1, cols - 1), (rows - 1, 0), (0, cols - 1), (0, 0)]):
-            value = field[row : row + 1, col : col + 1]
-            out_corner[place] = jnp.broadcast_to(value, (1, LANES))
+    def send_vector(ref, slot):
+        for side, near, far in ((0, rows - 1, rows - 2), (1, 0, 1)):
+            out_lon[0, side, 0] = ref[near : near + 1, :]
+            out_lon[0, side, 1] = ref[far : far + 1, :]
+        send_lon(0, slot)
+        for side, at in ((0, cols - LANES), (1, 0)):
+            near, far = ((0, 1), (LANES - 1, LANES - 2))[1 - side]
+            tile = ref[:, at : at + LANES]
+            out_lat[0, side, 0] = to_row(tile[:, near : near + 1])
+            out_lat[0, side, 1] = to_row(tile[:, far : far + 1])
+        send_lat(0, slot)
+        for place, (row, col) in enumerate(
+            [(rows - 1, cols - 1), (rows - 1, 0), (0, cols - 1), (0, 0)]
+        ):
+            value = ref[row : row + 1, col // LANES * LANES : col // LANES * LANES + LANES]
+            lane_at = col % LANES
+            out_corner[place] = jnp.broadcast_to(value[:, lane_at : lane_at + 1], (1, LANES))
+        send_corners(slot)
 
     def pack_coefficients(kappa, prior):
         for place, field in enumerate((kappa, prior)):
@@ -216,7 +226,7 @@
     def whole(ref, sem):
         pltpu.make_async_copy(ref, ref, sem).wait()
 
-    def send_sides(kind, slot):
+    def send_lon(kind, slot):
         for side, peer in enumerate((lon_next, lon_prev)):
             remote(
                 out_lon.at[kind, side],
@@ -225,6 +235,8 @@
                 edge_recv.at[slot, 0],
                 peer,
             ).start()
+
+    def send_lat(kind, slot):
         for side, peer in enumerate((lat_next, lat_prev)):
             remote(
                 out_lat.at[kind, side],
@@ -308,6 +320,7 @@
         lane_wide = lax.broadcasted_iota(jnp.int32, (1, cols), 1)
         lane_row = lax.broadcasted_iota(jnp.int32, (1, LANES), 1)
         present = (has_prev, has_next)
+        own = to_row(v_ref[:, 0:1]), to_row(v_ref[:, cols - 1 : cols])
         beside_lon, beside_lat = [], []
         for side, at in ((0, 0), (1, rows - 1)):
             near, far = edge_lon[turn, side, 0], edge_lon[turn, side, 1]
@@ -324,7 +337,7 @@
             first, last = edge_corner[turn, side][:, :1], edge_corner[turn, 2 + side][:, :1]
             west = jnp.where(lane_row == 0, first, pltpu.roll(near, 1, 1))
             east = jnp.where(lane_row == rows - 1, last, pltpu.roll(near, LANES - 1, 1))
-            around = far + out_lat[0, 1 - side, 0] + west + east
+            around = far + own[side] + west + east
             value = prior * ((kappa + 4.0) * near - around) * present[side]
             beside_lat.append(to_column(value, rows))
         scaled = u_ref[...]
@@ -350,7 +363,8 @@
     def one_turned(tile, carry):
         place = jnp.zeros((ROWS, LANES), jnp.int32)
         for block in range(PER_TILE):
-            place = jnp.where(chunk == block, lat_ref[0, tile * PER_TILE + block], place)
+            anchor = lat_ref[0, tile * PER_TILE + -block % PER_TILE]
+            place = jnp.where(chunk == block, anchor, place)
         place = (place + lane % PSIDE)[:1]
         start = pl.multiple_of(tile * LANES, LANES)
         turned_ref[:, pl.ds(start, LANES)] = jnp.where(cell == place, 1.0, 0.0).astype(BF16)
@@ -360,7 +374,7 @@
     for copy in loads[2:]:
         copy.wait()
     slot = lax.broadcasted_iota(jnp.int32, (blocks, reads), 0)
-    weights = jnp.where(slot < count_ref[0], weights_ref[...], 0.0)
+    weights = jnp.where(slot < count_ref[...], weights_ref[...], 0.0)
     weights_ref[...] = weights
     term_ref[...] = weights * readings_ref[...]
     ids_row = jnp.broadcast_to(ids_ref[...].astype(F32), (blocks, blocks))
@@ -379,11 +393,11 @@
             for half in range(2):
                 picked = jnp.zeros((ROWS, LANES), F32)
                 for place in range(PER_TILE):
-                    start = lon_ref[0, tile * PER_TILE + place] + half * ROWS
+                    start = lon_ref[0, tile * PER_TILE + -place % PER_TILE] + half * ROWS
                     window = columns_ref[tile, pl.ds(start, ROWS), :]
                     picked = jnp.where(chunk == place, window, picked)
                 halves.append(picked)
-            done = block_transpose(jnp.stack(halves))
+            done = turn_blocks(jnp.stack(halves))
             for half in range(2):
                 patch_ref[
                     tile * ROWS : (tile + 1) * ROWS, half * LANES : (half + 1) * LANES
@@ -418,7 +432,8 @@
         lead = rows - PSIDE
         for half in range(2):
             part = terms[:, half * LANES : (half + 1) * LANES].reshape(tiles, ROWS, LANES)
-            padded_ref[:, lead + half * ROWS : lead + (half + 1) * ROWS, :] = block_transpose(part)
+            part = negate_rows(turn_blocks(part))
+            padded_ref[:, lead + half * ROWS : lead + (half + 1) * ROWS, :] = part
         wide = lax.broadcasted_iota(jnp.int32, (rows, LANES), 1) // PSIDE
 
         def one_tile(tile, carry):
@@ -462,7 +477,7 @@
         def _():
             receive_sides(ITERS)
 
-        @pl.when(turn == 2)
+        @pl.when((turn > 0) & (turn < ITERS))
         def _():
             receive_sides(turn - 1)
 
@@ -470,16 +485,30 @@
         def _():
             inner_stencil(turn - 1)
             whole(edge_corner.at[turn - 1], corner_sem.at[turn - 1])
+
+            @pl.when(turn == ITERS)
+            def _():
+                edge_corner[2] = edge_corner[1] - first_ref[...] * edge_corner[2]
+
             image_ref[...] += outer_stencil(turn - 1)
             finish_sides(0)
             whole(out_corner, corner_sem.at[ITERS])
 
         @pl.when(turn == 0)
         def _():
+            pl.semaphore_wait(barrier, len(peers))
+
+        @pl.when(turn < ITERS)
+        def _():
+            send_vector(image_ref, turn)
+
+        @pl.when(turn == 0)
+        def _():
             right = image_ref[...]
             r0_ref[...] = right
             v_ref[...] = right
-            pl.semaphore_wait(barrier, len(peers))
+            send_lon(1, ITERS)
+            send_lat(1, ITERS)
 
         @pl.when(turn == 1)
         def _():
@@ -490,20 +519,18 @@
         @pl.when(turn == 2)
         def _():
             norm, curve = unpacked(receive_sum(first_b, first_b_sem), 2)
-            alpha = norm / curve
+            step = norm / curve
             w0 = w0_ref[...]
-            w1 = w0 - alpha * image_ref[...]
-            r1_ref[...] = r0_ref[...] - alpha * w0
+            w1 = w0 - step * image_ref[...]
+            r1_ref[...] = r0_ref[...] - step * w0
             w1_ref[...] = w1
             v_ref[...] = w1
-            lane_row = lane[:1]
-            first_ref[...] = jnp.where(lane_row == 0, alpha, jnp.where(lane_row == 1, curve, 0.0))
+            first_ref[...] = jnp.broadcast_to(step, (1, LANES))
 
         @pl.when(turn == ITERS)
         def _():
-            sizes = unpacked(receive_sum(last_b, last_b_sem), 7)
-            alpha, a = unpacked(first_ref[...], 2)
-            g0, g1, d, b, c, e, f = sizes
+            g0, g1, d, b, c, e, a, f = unpacked(receive_sum(last_b, last_b_sem), 8)
+            step = first_ref[:, 0:1]
             g2 = d
             l1, l2 = b / a, c / a
             d, e, f = d - l1 * b, e - l1 * c, f - l2 * c
@@ -515,19 +542,11 @@
             c1 = g1 / d - m * c2
             c0 = g0 / a - l1 * c1 - l2 * c2
             w1, r1 = w1_ref[...], r1_ref[...]
-            x_ref[...] = (alpha + c0) * r0_ref[...] + c1 * r1 + c2 * w1
+            x_ref[...] = (step + c0) * r0_ref[...] + c1 * r1 + c2 * w1
             r_ref[...] = r1 - c0 * w0_ref[...] - c1 * w1 - c2 * image_ref[...]
 
         @pl.when(turn < ITERS)
         def _():
-            pack_vector(v_ref[...])
-            send_sides(0, turn)
-            send_corners(turn)
-
-            @pl.when(turn == 0)
-            def _():
-                send_sides(1, ITERS)
-
             gather(v_ref[...])
 
             @pl.when(turn == 1)
@@ -546,19 +565,20 @@
 
             @pl.when(turn == 0)
             def _():
-                inside, lon_sides, lat_sides = curve()
-                parts = [fold(r0_ref[...] * r0_ref[...]), inside]
-                receive_sides(turn)
-                first_a[me_a] = packed(parts, side_square(turn, lon_sides, lat_sides))
+                parts = [fold(r0_ref[...] * r0_ref[...]), curve()[0]]
+                first_a[me_a] = packed(parts, jnp.zeros((1, LANES), F32))
                 send_sum(first_a, me_a, first_a_sem, peers_a)
 
             @pl.when(turn == 2)
             def _():
                 r0, w0, r1, w1 = r0_ref[...], w0_ref[...], r1_ref[...], w1_ref[...]
-                pairs = [(r0, r1), (r1, r1), (r1, w1), (r0, w1), (w0, w1), (w1, w1)]
+                pairs = [(r0, r1), (r1, r1), (r1, w1), (r0, w1), (w0, w1), (w1, w1), (r0, w0)]
                 inside, lon_sides, lat_sides = curve()
                 parts = [fold(one * two) for one, two in pairs] + [inside]
                 receive_sides(turn)
+                step = first_ref[:, 0:1]
+                edge_lon[2] = edge_lon[1] - step * edge_lon[2]
+                edge_lat[2] = edge_lat[1] - step * edge_lat[2]
                 last_a[core] = packed(parts, side_square(turn, lon_sides, lat_sides))
                 send_sum(last_a, core, last_a_sem, [twin])
                 last_b[me_far] = receive_sum(last_a, last_a_sem)
@@ -637,7 +657,7 @@
             plane,
             plane,
             pltpu.VMEM((kinds, reads, cells), BF16),
-            pltpu.SMEM((1,), jnp.int32),
+            pltpu.VMEM((1, 1), jnp.int32),
             pltpu.SMEM((1, blocks), jnp.int32),
             pltpu.SMEM((1, blocks), jnp.int32),
             pltpu.VMEM((1, blocks), jnp.int32),
@@ -686,7 +706,7 @@
         kappa_sq,
         prior_scale,
         templates,
-        block_counts,
+        block_counts.reshape(1, 1),
         anchor_lon,
         anchor_lat,
         template_ids,

time: 36.1 us -> 33.9 us (0.939); the launches traced: 35.5 us -> 33.8 us
  Pallas kernels: 34.2 us -> 32.5 us
    pallas_call x1, Pallas kernels: 33.5 us -> 31.8 us  [on_device(): pl.pallas_call(functools.partial(kernel, n_lon, n_lat), out_shape=(pltpu....]
where the time goes in v6:
time: 33.9 us; the launch traced here: 33.8 us
  Pallas kernels  32.5 us (96%)
  between operations  1.29 us (4%)
    pallas_call x1, Pallas kernels, on_device(): pl.pallas_call(functools.partial(kernel, n_lon, n_lat), out_shape=(pltpu....  31.8 us
    pallas_call x1, Pallas kernels, on_device(): pl.pallas_call(hand_out, out_shape=(field, field), in_specs=[pl.BlockSpec...  0.72 us

profile of v6, /device:TPU:1, one launch (start us, length us, event | category | flops | bytes accessed | tf_op | source)
XLA Modules:
  0.0 33.8 jit_solution(11098228764727346127)
XLA Ops:
  1.3 31.8 %shard_map.104 = (f32[64,512]{1,0:T(8,128)S(1)}, f32[64,512]{1,0:T(8,128)S(1)}) custom-call(f32[64,512]{1,0:T(8,128)} %kappa_hbm.1, f32[64,512]{1,0:T(8,128)} %prior_hbm.1, bf16[64,128,256]{2,1,0:T(8,128)(2,1)} %templates_hbm.1, s32[1,1]{1,0:T(1,128)} %bitcast.3.count_hbm, s32[1,128]{1,0:T(1,128)} %lon_hbm.1, s32[1,128]{1,0:T(1,128)} %lat_hbm.1, ...), custom_call_target="tpu_custom_call" | custom-call | tf_op jit(solution)/shard_map/pallas_call | solution.py:651
  33.1 0.7 %shard_map.105 = (f32[64,512]{1,0:T(8,128)}, f32[64,512]{1,0:T(8,128)}) custom-call(f32[64,512]{1,0:T(8,128)S(1)} %get-tuple-element.4.x_in, f32[64,512]{1,0:T(8,128)S(1)} %get-tuple-element.5.r_in), custom_call_target="tpu_custom_call" | custom-call | tf_op jit(solution)/shard_map/pallas_call | solution.py:716

commit v7 on v6

--- a/solution.py
+++ b/solution.py
@@ -9,6 +9,7 @@
 
 PSIDE = 16
 ITERS = 3
+PART = 16
 LANES = 128
 ROWS = 8
 PER_TILE = LANES // PSIDE
@@ -105,10 +106,10 @@
     turned_ref,
     columns_ref,
     padded_ref,
-    spread_ref,
     patch_ref,
     ids_rows_ref,
     term_ref,
+    terms_ref,
     r0_ref,
     w0_ref,
     r1_ref,
@@ -117,7 +118,8 @@
     v_ref,
     u_ref,
     first_ref,
-    curve_ref,
+    pairs_ref,
+    own_ref,
     out_lon,
     out_lat,
     out_corner,
@@ -129,6 +131,7 @@
     last_a,
     last_b,
     load_sem,
+    template_sem,
     edge_send,
     edge_recv,
     corner_sem,
@@ -150,18 +153,28 @@
         for place, (source, target) in enumerate(
             [
                 (lat_hbm, lat_ref),
-                (templates_hbm, templates_ref),
-                (lon_hbm, lon_ref),
                 (ids_hbm, ids_ref),
                 (count_hbm, count_ref),
                 (noise_hbm, weights_ref),
                 (readings_hbm, readings_ref),
+                (lon_hbm, lon_ref),
                 (kappa_hbm, kappa_ref),
                 (prior_hbm, prior_ref),
             ]
         )
     ]
-    for copy in loads:
+
+    def template_part(part):
+        some = pl.ds(part * PART, PART)
+        return pltpu.make_async_copy(
+            templates_hbm.at[some], templates_ref.at[some], template_sem.at[part]
+        )
+
+    for copy in loads[:5]:
+        copy.start()
+    for part in range(kinds // PART):
+        template_part(part).start()
+    for copy in loads[5:]:
         copy.start()
 
     me_a = lat * 2 + core
@@ -280,16 +293,17 @@
     has_prev = (lat > 0).astype(F32)
     has_next = (lat < n_lat - 1).astype(F32)
 
-    def inner_stencil(turn):
-        field = v_ref[...]
-        around = shifted(
-            field,
-            edge_lon[turn, 0, 0],
-            edge_lon[turn, 1, 0],
-            to_column(edge_lat[turn, 0, 0] * has_prev, rows),
-            to_column(edge_lat[turn, 1, 0] * has_next, rows),
-        )
-        u_ref[...] = prior_ref[...] * ((kappa_ref[...] + 4.0) * field - around)
+    def complete_inner(turn):
+        for side, at in ((0, 0), (1, rows - 1)):
+            change = prior_ref[at : at + 1, :] * edge_lon[turn, side, 0]
+            u_ref[at : at + 1, :] = u_ref[at : at + 1, :] - change
+        lane_tile = lax.broadcasted_iota(jnp.int32, (rows, LANES), 1)
+        for side, (at, end, present) in enumerate(
+            ((0, 0, has_prev), (cols - LANES, LANES - 1, has_next))
+        ):
+            beside = to_column(edge_lat[turn, side, 0] * present, rows)
+            change = prior_ref[:, at : at + LANES] * jnp.where(lane_tile == end, beside, 0.0)
+            u_ref[:, at : at + LANES] = u_ref[:, at : at + LANES] - change
 
     def inner_square():
         field = v_ref[...]
@@ -298,7 +312,11 @@
         inner = (kappa_ref[...] + 4.0) * field - around
         lon_sides = inner[0:1, :], inner[rows - 1 : rows, :]
         lat_sides = to_row(inner[:, 0:1]), to_row(inner[:, cols - 1 : cols])
-        return fold(prior_ref[...] * inner * inner), lon_sides, lat_sides
+        scaled = prior_ref[...] * inner
+        u_ref[...] = scaled
+        own_ref[0] = to_row(field[:, 0:1])
+        own_ref[1] = to_row(field[:, cols - 1 : cols])
+        return fold(scaled * inner), lon_sides, lat_sides
 
     def side_square(turn, lon_sides, lat_sides):
         lane_row = lax.broadcasted_iota(jnp.int32, (1, LANES), 1)
@@ -320,7 +338,6 @@
         lane_wide = lax.broadcasted_iota(jnp.int32, (1, cols), 1)
         lane_row = lax.broadcasted_iota(jnp.int32, (1, LANES), 1)
         present = (has_prev, has_next)
-        own = to_row(v_ref[:, 0:1]), to_row(v_ref[:, cols - 1 : cols])
         beside_lon, beside_lat = [], []
         for side, at in ((0, 0), (1, rows - 1)):
             near, far = edge_lon[turn, side, 0], edge_lon[turn, side, 1]
@@ -337,7 +354,7 @@
             first, last = edge_corner[turn, side][:, :1], edge_corner[turn, 2 + side][:, :1]
             west = jnp.where(lane_row == 0, first, pltpu.roll(near, 1, 1))
             east = jnp.where(lane_row == rows - 1, last, pltpu.roll(near, LANES - 1, 1))
-            around = far + own[side] + west + east
+            around = far + own_ref[side] + west + east
             value = prior * ((kappa + 4.0) * near - around) * present[side]
             beside_lat.append(to_column(value, rows))
         scaled = u_ref[...]
@@ -348,19 +365,15 @@
         jnp.int32, (PSIDE, cols), 0
     )
 
-    def one_selector(block, carry):
-        start = pl.multiple_of(block * PSIDE, PSIDE)
-        chosen = jnp.where(offset == lat_ref[0, block], 1.0, 0.0)
-        select_ref[pl.ds(start, PSIDE), :] = chosen.astype(BF16)
-        return carry
-
-    loads[0].wait()
-    lax.fori_loop(0, blocks, one_selector, 0, unroll=16)
     lane = lax.broadcasted_iota(jnp.int32, (ROWS, LANES), 1)
     chunk = lane // PSIDE
     cell = lax.broadcasted_iota(jnp.int32, (cols, LANES), 0)
 
-    def one_turned(tile, carry):
+    def selectors(tile):
+        for block in range(PER_TILE):
+            start = pl.multiple_of((tile * PER_TILE + block) * PSIDE, PSIDE)
+            chosen = jnp.where(offset == lat_ref[0, tile * PER_TILE + block], 1.0, 0.0)
+            select_ref[pl.ds(start, PSIDE), :] = chosen.astype(BF16)
         place = jnp.zeros((ROWS, LANES), jnp.int32)
         for block in range(PER_TILE):
             anchor = lat_ref[0, tile * PER_TILE + -block % PER_TILE]
@@ -368,27 +381,57 @@
         place = (place + lane % PSIDE)[:1]
         start = pl.multiple_of(tile * LANES, LANES)
         turned_ref[:, pl.ds(start, LANES)] = jnp.where(cell == place, 1.0, 0.0).astype(BF16)
-        return carry
-
-    lax.fori_loop(0, tiles, one_turned, 0, unroll=2)
-    for copy in loads[2:]:
+
+    def twice(value):
+        return jnp.concatenate([value, value], 0)
+
+    def one_product(both, ids, first, count):
+        left = [
+            jnp.where(ids == jnp.asarray(first + kind).astype(BF16), both, jnp.zeros_like(both))
+            for kind in range(count)
+        ]
+        table = templates_ref[pl.ds(first, count)].reshape(count * reads, cells)
+        return jnp.dot(jnp.concatenate(left, 1), table, preferred_element_type=F32)
+
+    for copy in loads[:5]:
         copy.wait()
     slot = lax.broadcasted_iota(jnp.int32, (blocks, reads), 0)
     weights = jnp.where(slot < count_ref[...], weights_ref[...], 0.0)
     weights_ref[...] = weights
-    term_ref[...] = weights * readings_ref[...]
     ids_row = jnp.broadcast_to(ids_ref[...].astype(F32), (blocks, blocks))
-    ids_rows_ref[...] = jnp.transpose(ids_row)
+    ids_rows = jnp.transpose(ids_row)
+    ids_rows_ref[...] = ids_rows
+    weighted = jnp.concatenate(split(weights * readings_ref[...]), 0)
+    ids_twice = twice(ids_rows.astype(BF16))
+    terms_ref[...] = jnp.zeros(terms_ref.shape, F32)
+    for ref in (r0_ref, w0_ref, r1_ref, w1_ref):
+        ref[...] = jnp.zeros(ref.shape, F32)
+    parts = kinds // PART
+
+    def one_part(part, carry):
+        template_part(part).wait()
+        terms_ref[...] += one_product(weighted, ids_twice, part * PART, PART)
+        for tile in range(tiles // parts):
+            selectors(part * (tiles // parts) + tile)
+        return carry
+
+    lax.fori_loop(0, parts, one_part, 0)
+    for copy in loads[5:]:
+        copy.wait()
 
     def gather(field):
-        high, low = split(field)
-        both = jnp.dot(
-            jnp.concatenate([high, low], 0), turned_ref[...], preferred_element_type=F32
-        )
-        both = both[:rows] + both[rows:]
-        for tile in range(tiles):
-            columns_ref[tile] = both[:, tile * LANES : (tile + 1) * LANES]
-        for tile in range(tiles):
+        field = jnp.concatenate(split(field), 0)
+        some = 4
+        for first in range(0, tiles, some):
+            beside = turned_ref[:, first * LANES : (first + some) * LANES]
+            both = jnp.dot(field, beside, preferred_element_type=F32)
+            both = both[:rows] + both[rows:]
+            for tile in range(some):
+                columns_ref[first + tile] = both[:, tile * LANES : (tile + 1) * LANES]
+            pick(first, some)
+
+    def pick(first, some):
+        for tile in range(first, first + some):
             halves = []
             for half in range(2):
                 picked = jnp.zeros((ROWS, LANES), F32)
@@ -414,20 +457,18 @@
             acc = jnp.where((ids == kind)[:1], result, acc)
         return jnp.transpose(acc[:, :blocks] + acc[:, blocks:])
 
-    def spread(mixed):
-        high, low = split(mixed)
-        both = jnp.concatenate([high, low], 0)
-        ids = ids_rows_ref[...].astype(BF16)
-        ids = jnp.concatenate([ids, ids], 0)
-        terms = jnp.zeros((2 * blocks, cells), F32)
-        some = 8
-        for first in range(0, kinds, some):
-            left = [
-                jnp.where(ids == kind, both, jnp.zeros_like(both))
-                for kind in range(first, first + some)
-            ]
-            table = templates_ref[first : first + some].reshape(some * reads, cells)
-            terms += jnp.dot(jnp.concatenate(left, 1), table, preferred_element_type=F32)
+    def spread(turn):
+        @pl.when(turn > 0)
+        def _():
+            both = jnp.concatenate(split(term_ref[...]), 0)
+            ids = twice(ids_rows_ref[...].astype(BF16))
+            terms = jnp.zeros((2 * blocks, cells), F32)
+            some = 8
+            for first in range(0, kinds, some):
+                terms += one_product(both, ids, first, some)
+            terms_ref[...] = terms
+
+        terms = terms_ref[...]
         terms = terms[:blocks] + terms[blocks:]
         lead = rows - PSIDE
         for half in range(2):
@@ -436,20 +477,17 @@
             padded_ref[:, lead + half * ROWS : lead + (half + 1) * ROWS, :] = part
         wide = lax.broadcasted_iota(jnp.int32, (rows, LANES), 1) // PSIDE
 
-        def one_tile(tile, carry):
+        placed = []
+        for tile in range(tiles):
             picked = jnp.zeros((rows, LANES), F32)
             for place in range(PER_TILE):
                 start = lead - lon_ref[0, tile * PER_TILE + place]
                 window = padded_ref[tile, pl.ds(start, rows), :]
                 picked = jnp.where(wide == place, window, picked)
-            high, low = split(picked)
-            start = pl.multiple_of(tile * LANES, LANES)
-            spread_ref[0:rows, pl.ds(start, LANES)] = high
-            spread_ref[rows : 2 * rows, pl.ds(start, LANES)] = low
-            return carry
-
-        lax.fori_loop(0, tiles, one_tile, 0, unroll=tiles)
-        both = jnp.dot(spread_ref[...], select_ref[...], preferred_element_type=F32)
+            placed.append(jnp.concatenate(split(picked), 0))
+        both = jnp.dot(
+            jnp.concatenate(placed, 1), select_ref[...], preferred_element_type=F32
+        )
         return both[:rows] + both[rows:]
 
     row_at = lax.broadcasted_iota(jnp.int32, (ROWS, LANES), 0)
@@ -468,10 +506,9 @@
         ]
 
     pack_coefficients(kappa_ref[...], prior_ref[...])
-    loads[1].wait()
 
     def one_turn(turn, carry):
-        image_ref[...] = spread(term_ref[...])
+        image_ref[...] = spread(turn)
 
         @pl.when(turn == 1)
         def _():
@@ -483,7 +520,7 @@
 
         @pl.when(turn > 0)
         def _():
-            inner_stencil(turn - 1)
+            complete_inner(turn - 1)
             whole(edge_corner.at[turn - 1], corner_sem.at[turn - 1])
 
             @pl.when(turn == ITERS)
@@ -554,27 +591,25 @@
                 first_b[chip] = receive_sum(first_a, first_a_sem)
                 send_sum(first_b, chip, first_b_sem, peers_b)
 
+            inside, lon_sides, lat_sides = inner_square()
+            r0, w0, r1, w1 = r0_ref[...], w0_ref[...], r1_ref[...], w1_ref[...]
+            pairs = [(r0, r1), (r1, r1), (r1, w1), (r0, w1), (w0, w1), (w1, w1), (r0, w0)]
+            for place, (one, two) in enumerate(pairs):
+                pairs_ref[place] = fold(one * two)
             image = read()
             mixed = weights_ref[...] * image
             term_ref[...] = mixed
-            curve_ref[...] = fold(mixed * image)
-
-            def curve():
-                inside, lon_sides, lat_sides = inner_square()
-                return curve_ref[...] + inside, lon_sides, lat_sides
+            pairs_ref[len(pairs)] = inside + fold(mixed * image)
 
             @pl.when(turn == 0)
             def _():
-                parts = [fold(r0_ref[...] * r0_ref[...]), curve()[0]]
+                parts = [fold(r0_ref[...] * r0_ref[...]), pairs_ref[7]]
                 first_a[me_a] = packed(parts, jnp.zeros((1, LANES), F32))
                 send_sum(first_a, me_a, first_a_sem, peers_a)
 
             @pl.when(turn == 2)
             def _():
-                r0, w0, r1, w1 = r0_ref[...], w0_ref[...], r1_ref[...], w1_ref[...]
-                pairs = [(r0, r1), (r1, r1), (r1, w1), (r0, w1), (w0, w1), (w1, w1), (r0, w0)]
-                inside, lon_sides, lat_sides = curve()
-                parts = [fold(one * two) for one, two in pairs] + [inside]
+                parts = [pairs_ref[place] for place in range(8)]
                 receive_sides(turn)
                 step = first_ref[:, 0:1]
                 edge_lon[2] = edge_lon[1] - step * edge_lon[2]
@@ -667,10 +702,10 @@
             pltpu.VMEM((cols, blocks * PSIDE), BF16),
             pltpu.VMEM((tiles, rows, LANES), F32),
             pltpu.VMEM((tiles, 2 * rows - PSIDE, LANES), F32),
-            pltpu.VMEM((2 * rows, blocks * PSIDE), BF16),
             pltpu.VMEM((blocks, cells), F32),
             pltpu.VMEM((blocks, blocks), F32),
             pltpu.VMEM((blocks, reads), F32),
+            pltpu.VMEM((2 * blocks, cells), F32),
             plane,
             plane,
             plane,
@@ -679,7 +714,8 @@
             plane,
             plane,
             pltpu.VMEM((1, LANES), F32),
-            pltpu.VMEM((ROWS, LANES), F32),
+            pltpu.VMEM((8, ROWS, LANES), F32),
+            pltpu.VMEM((2, 1, LANES), F32),
             pltpu.VMEM((2, 2, 2, 1, cols), F32),
             pltpu.VMEM((2, 2, 2, 1, LANES), F32),
             pltpu.VMEM((4, 1, LANES), F32),
@@ -690,7 +726,8 @@
             pltpu.VMEM((chips_lon, 1, LANES), F32),
             pltpu.VMEM((2, 1, LANES), F32),
             pltpu.VMEM((chips, 1, LANES), F32),
-            dma((9,)),
+            dma((8,)),
+            dma((kinds // PART,)),
             dma((2, 2)),
             dma((ITERS + 1, 2)),
             dma((ITERS + 1,)),

time: 33.9 us -> 33.3 us (0.982)
  Pallas kernels: 32.5 us -> 31.9 us
    pallas_call x1, Pallas kernels: 31.8 us -> 31.2 us  [on_device(): pl.pallas_call(functools.partial(kernel, n_lon, n_lat), out_shape=(pltpu....]
where the time goes in v7:
time: 33.3 us; the launch traced here: 33.2 us
  Pallas kernels  31.9 us (96%)
  between operations  1.29 us (4%)
    pallas_call x1, Pallas kernels, on_device(): pl.pallas_call(functools.partial(kernel, n_lon, n_lat), out_shape=(pltpu....  31.2 us
    pallas_call x1, Pallas kernels, on_device(): pl.pallas_call(hand_out, out_shape=(field, field), in_specs=[pl.BlockSpec...  0.72 us

profile of v7, /device:TPU:1, one launch (start us, length us, event | category | flops | bytes accessed | tf_op | source)
XLA Modules:
  0.0 33.2 jit_solution(2911712264490633831)
XLA Ops:
  1.3 31.2 %shard_map.104 = (f32[64,512]{1,0:T(8,128)S(1)}, f32[64,512]{1,0:T(8,128)S(1)}) custom-call(f32[64,512]{1,0:T(8,128)} %kappa_hbm.1, f32[64,512]{1,0:T(8,128)} %prior_hbm.1, bf16[64,128,256]{2,1,0:T(8,128)(2,1)} %templates_hbm.1, s32[1,1]{1,0:T(1,128)} %bitcast.3.count_hbm, s32[1,128]{1,0:T(1,128)} %lon_hbm.1, s32[1,128]{1,0:T(1,128)} %lat_hbm.1, ...), custom_call_target="tpu_custom_call" | custom-call | tf_op jit(solution)/shard_map/pallas_call | solution.py:686
  32.5 0.7 %shard_map.105 = (f32[64,512]{1,0:T(8,128)}, f32[64,512]{1,0:T(8,128)}) custom-call(f32[64,512]{1,0:T(8,128)S(1)} %get-tuple-element.4.x_in, f32[64,512]{1,0:T(8,128)S(1)} %get-tuple-element.5.r_in), custom_call_target="tpu_custom_call" | custom-call | tf_op jit(solution)/shard_map/pallas_call | solution.py:753

commit v8 on v7

--- a/solution.py
+++ b/solution.py
@@ -393,6 +393,9 @@
         table = templates_ref[pl.ds(first, count)].reshape(count * reads, cells)
         return jnp.dot(jnp.concatenate(left, 1), table, preferred_element_type=F32)
 
+    terms_ref[...] = jnp.zeros(terms_ref.shape, F32)
+    for ref in (r0_ref, w0_ref, r1_ref, w1_ref):
+        ref[...] = jnp.zeros(ref.shape, F32)
     for copy in loads[:5]:
         copy.wait()
     slot = lax.broadcasted_iota(jnp.int32, (blocks, reads), 0)
@@ -403,9 +406,6 @@
     ids_rows_ref[...] = ids_rows
     weighted = jnp.concatenate(split(weights * readings_ref[...]), 0)
     ids_twice = twice(ids_rows.astype(BF16))
-    terms_ref[...] = jnp.zeros(terms_ref.shape, F32)
-    for ref in (r0_ref, w0_ref, r1_ref, w1_ref):
-        ref[...] = jnp.zeros(ref.shape, F32)
     parts = kinds // PART
 
     def one_part(part, carry):
@@ -492,9 +492,8 @@
 
     row_at = lax.broadcasted_iota(jnp.int32, (ROWS, LANES), 0)
 
-    def packed(parts, more):
+    def packed(parts):
         parts = [jnp.sum(part, axis=0, keepdims=True) for part in parts]
-        parts[-1] = parts[-1] + more
         parts += [jnp.zeros((1, LANES), F32)] * (ROWS - len(parts))
         total = jnp.sum(jnp.concatenate(parts, 0), axis=1, keepdims=True)
         return jnp.sum(jnp.where(row_at == lane, total, 0.0), axis=0, keepdims=True)
@@ -604,17 +603,19 @@
             @pl.when(turn == 0)
             def _():
                 parts = [fold(r0_ref[...] * r0_ref[...]), pairs_ref[7]]
-                first_a[me_a] = packed(parts, jnp.zeros((1, LANES), F32))
+                first_a[me_a] = packed(parts)
                 send_sum(first_a, me_a, first_a_sem, peers_a)
 
             @pl.when(turn == 2)
             def _():
-                parts = [pairs_ref[place] for place in range(8)]
+                known = packed([pairs_ref[place] for place in range(8)])
                 receive_sides(turn)
                 step = first_ref[:, 0:1]
                 edge_lon[2] = edge_lon[1] - step * edge_lon[2]
                 edge_lat[2] = edge_lat[1] - step * edge_lat[2]
-                last_a[core] = packed(parts, side_square(turn, lon_sides, lat_sides))
+                more = side_square(turn, lon_sides, lat_sides)
+                more = jnp.sum(more, axis=1, keepdims=True)
+                last_a[core] = known + jnp.where(lane[:1] == 7, more, 0.0)
                 send_sum(last_a, core, last_a_sem, [twin])
                 last_b[me_far] = receive_sum(last_a, last_a_sem)
                 send_sum(last_b, me_far, last_b_sem, peers_far)

time: 33.3 us -> 33.3 us (level)
  no operation moved by 1% of the time
where the time goes in v8:
time: 33.3 us; the launch traced here: 33.2 us
  Pallas kernels  31.9 us (96%)
  between operations  1.29 us (4%)
    pallas_call x1, Pallas kernels, on_device(): pl.pallas_call(functools.partial(kernel, n_lon, n_lat), out_shape=(pltpu....  31.2 us
    pallas_call x1, Pallas kernels, on_device(): pl.pallas_call(hand_out, out_shape=(field, field), in_specs=[pl.BlockSpec...  0.72 us

profile of v8, /device:TPU:1, one launch (start us, length us, event | category | flops | bytes accessed | tf_op | source)
XLA Modules:
  0.0 33.2 jit_solution(4242629100464697286)
XLA Ops:
  1.3 31.2 %shard_map.104 = (f32[64,512]{1,0:T(8,128)S(1)}, f32[64,512]{1,0:T(8,128)S(1)}) custom-call(f32[64,512]{1,0:T(8,128)} %kappa_hbm.1, f32[64,512]{1,0:T(8,128)} %prior_hbm.1, bf16[64,128,256]{2,1,0:T(8,128)(2,1)} %templates_hbm.1, s32[1,1]{1,0:T(1,128)} %bitcast.3.count_hbm, s32[1,128]{1,0:T(1,128)} %lon_hbm.1, s32[1,128]{1,0:T(1,128)} %lat_hbm.1, ...), custom_call_target="tpu_custom_call" | custom-call | tf_op jit(solution)/shard_map/pallas_call | solution.py:687
  32.5 0.7 %shard_map.105 = (f32[64,512]{1,0:T(8,128)}, f32[64,512]{1,0:T(8,128)}) custom-call(f32[64,512]{1,0:T(8,128)S(1)} %get-tuple-element.4.x_in, f32[64,512]{1,0:T(8,128)S(1)} %get-tuple-element.5.r_in), custom_call_target="tpu_custom_call" | custom-call | tf_op jit(solution)/shard_map/pallas_call | solution.py:754

commit v9 on v8

--- a/solution.py
+++ b/solution.py
@@ -416,6 +416,7 @@
         return carry
 
     lax.fori_loop(0, parts, one_part, 0)
+    terms_ref[0:blocks, :] += terms_ref[blocks : 2 * blocks, :]
     for copy in loads[5:]:
         copy.wait()
 
@@ -466,10 +467,9 @@
             some = 8
             for first in range(0, kinds, some):
                 terms += one_product(both, ids, first, some)
-            terms_ref[...] = terms
-
-        terms = terms_ref[...]
-        terms = terms[:blocks] + terms[blocks:]
+            terms_ref[0:blocks, :] = terms[:blocks] + terms[blocks:]
+
+        terms = terms_ref[0:blocks, :]
         lead = rows - PSIDE
         for half in range(2):
             part = terms[:, half * LANES : (half + 1) * LANES].reshape(tiles, ROWS, LANES)

time: 33.3 us -> 33.3 us (level)
  no operation moved by 1% of the time
where the time goes in v9:
time: 33.3 us; the launch traced here: 33.2 us
  Pallas kernels  31.9 us (96%)
  between operations  1.29 us (4%)
    pallas_call x1, Pallas kernels, on_device(): pl.pallas_call(functools.partial(kernel, n_lon, n_lat), out_shape=(pltpu....  31.2 us
    pallas_call x1, Pallas kernels, on_device(): pl.pallas_call(hand_out, out_shape=(field, field), in_specs=[pl.BlockSpec...  0.72 us

profile of v9, /device:TPU:1, one launch (start us, length us, event | category | flops | bytes accessed | tf_op | source)
XLA Modules:
  0.0 33.2 jit_solution(15402358807069231074)
XLA Ops:
  1.3 31.2 %shard_map.104 = (f32[64,512]{1,0:T(8,128)S(1)}, f32[64,512]{1,0:T(8,128)S(1)}) custom-call(f32[64,512]{1,0:T(8,128)} %kappa_hbm.1, f32[64,512]{1,0:T(8,128)} %prior_hbm.1, bf16[64,128,256]{2,1,0:T(8,128)(2,1)} %templates_hbm.1, s32[1,1]{1,0:T(1,128)} %bitcast.3.count_hbm, s32[1,128]{1,0:T(1,128)} %lon_hbm.1, s32[1,128]{1,0:T(1,128)} %lat_hbm.1, ...), custom_call_target="tpu_custom_call" | custom-call | tf_op jit(solution)/shard_map/pallas_call | solution.py:687
  32.5 0.7 %shard_map.105 = (f32[64,512]{1,0:T(8,128)}, f32[64,512]{1,0:T(8,128)}) custom-call(f32[64,512]{1,0:T(8,128)S(1)} %get-tuple-element.4.x_in, f32[64,512]{1,0:T(8,128)S(1)} %get-tuple-element.5.r_in), custom_call_target="tpu_custom_call" | custom-call | tf_op jit(solution)/shard_map/pallas_call | solution.py:754
